TPU v7x, 32 devices: a whole 2x2x4 slice. The times are simulated.
32 devices in a mesh: groups: 2 (over y), seq: 8 (over z, x), head: 2 (over core).
Axes of the slice: x: 2, y: 2, z: 4, core: 2. Of those that a mesh axis runs over, the one named last changes fastest.
Arguments:
- cache_pool: bfloat16 [768, 128, 576], P(('groups', 'seq')), parts along dimension 0, may hold values from -6 to 6, as said below
- page_table: int32 [4, 128], P('groups'), parts along dimension 0, may hold values from -1 to 383, as said below
- prompt_len: int32 [4], P('groups'), parts along dimension 0, may hold values from 2048 to 16384, as said below
- host_samples: int32 [32], P(('groups', 'seq')), parts along dimension 0, may hold values from 0 to 15, as said below
- queries: bfloat16 [32, 2, 64, 576], P(('groups', 'seq'), None, 'head'), parts along dimension 0, may hold values from -82 to 82
- new_hidden: bfloat16 [32, 2, 7168], P(('groups', 'seq'), None, 'head'), parts along dimension 0, may hold values from -6 to 6
- kv_down: bfloat16 [7168, 576], P('head'), may hold values from -0.0625 to 0.0625
- kv_gain: float32 [512], replicated, may hold values from 0.1 to 1.9
- value_up: bfloat16 [64, 512, 128], P('head'), may hold values from -0.5 to 0.5
Outputs:
- new_rows: bfloat16 [32, 2, 576], P(('groups', 'seq')), parts along dimension 0
- attended: bfloat16 [32, 2, 64, 128], P(('groups', 'seq'), None, 'head'), parts along dimension 0
There are 2 independent parts, one for each index of `groups`. A program takes and returns all parts, laid end to end along the dimension named above; an argument that names none is the same for every part. Nothing has to cross between parts.
Inputs may be any that keep to these rules, and one draw needn't show every extreme that they name: `page_table`: row p lists the pool pages of prompt p in order, entry j holding its positions j * 128 to j * 128 + 127; after its first ceil(prompt_len[p] / 128) entries it is -1; no pool page is listed twice. Pool page q is row q % 48 of the seq device q // 48. `prompt_len`: one prompt has exactly 16384 tokens, every other one at most 16384. `host_samples`: each sample appears once. Sample s is fork s % 8 of prompt s // 8; slot i is served by the seq device i // 2. `cache_pool`: pool pages that no prompt lists hold arbitrary values.
All inputs are finite; a program needn't handle non-finite values.
Results may differ from a plain program's by a relative error of at most 0.003.
Values may be sent and summed in bfloat16 or wider, within the bound.
A program may use at most 128 MiB of HBM per device.

v0:
```python
import jax
import jax.numpy as jnp
from jax import lax
from jax.sharding import PartitionSpec as P

eps = 1e-06
score_scale = 192.0 ** (-0.5)
floor_score = -1e30


def finish_rows(raw_rows, row_gain):
    latent_width = row_gain.shape[0]
    latent = raw_rows[..., :latent_width]
    spread = lax.rsqrt(jnp.mean(latent * latent, axis=-1, keepdims=True) + eps)
    normed = latent * spread * row_gain
    return jnp.concatenate([normed, raw_rows[..., latent_width:]], axis=-1).astype(jnp.bfloat16)


def on_device(
    cache_pool,
    page_table,
    prompt_len,
    host_samples,
    queries,
    new_hidden,
    kv_down,
    kv_gain,
    value_up,
):
    slot_count = queries.shape[0]
    head_count = queries.shape[2]
    row_width = queries.shape[3]
    latent_width = kv_gain.shape[0]
    page_count = cache_pool.shape[0]
    page_rows = cache_pool.shape[1]
    prompts = page_table.shape[0]
    table_width = page_table.shape[1]
    samples = slot_count * lax.axis_size("seq")
    fork_count = samples // prompts
    block_rows = fork_count * 2 * head_count
    raw_part = jnp.dot(new_hidden, kv_down, preferred_element_type=jnp.float32)
    new_rows = finish_rows(lax.psum(raw_part, "head"), kv_gain)
    all_queries, all_samples = (
        lax.all_gather(queries, "seq", axis=0, tiled=True),
        lax.all_gather(host_samples, "seq", axis=0, tiled=True),
    )
    sample_ids = jnp.arange(samples, dtype=jnp.int32)
    matches = all_samples[None, :] == sample_ids[:, None]
    slot_index = jnp.sum(jnp.where(matches, sample_ids[None, :], 0), axis=1)
    query_prompt = all_queries[slot_index].reshape(prompts, block_rows, row_width)
    global_ids = lax.axis_index("seq") * page_count + jnp.arange(page_count, dtype=jnp.int32)
    matches_page = page_table[None, :, :] == global_ids[:, None, None]
    prompt_ids = jnp.arange(prompts, dtype=jnp.int32)
    page_live = jnp.any(matches_page, axis=(1, 2))
    page_prompt = jnp.sum(jnp.where(matches_page, prompt_ids[None, :, None], 0), axis=(1, 2))
    column_ids = jnp.arange(table_width, dtype=jnp.int32)
    page_number = jnp.sum(jnp.where(matches_page, column_ids[None, None, :], 0), axis=(1, 2))
    prompt_hot = page_prompt[:, None] == prompt_ids[None, :]
    page_length = jnp.sum(jnp.where(prompt_hot, prompt_len[None, :], 0), axis=1)
    live_rows = jnp.where(page_live, page_length - page_number * page_rows, 0)

    def score_page(carry, inputs):
        page_keys, prompt_pick, live_count = inputs
        query_block = lax.dynamic_index_in_dim(query_prompt, prompt_pick, 0, keepdims=False)
        scores = (
            lax.dot_general(
                query_block, page_keys, (((1,), (1,)), ((), ())), preferred_element_type=jnp.float32
            )
            * score_scale
        )
        inside = jnp.arange(page_rows, dtype=jnp.int32) < live_count
        return (carry, jnp.where(inside[None, :], scores, floor_score))

    _, all_scores = lax.scan(score_page, 0, (cache_pool, page_prompt, live_rows))
    page_top = jnp.max(all_scores, axis=2)
    local_top = jnp.max(
        jnp.where(prompt_hot[:, :, None], page_top[:, None, :], floor_score), axis=0
    )
    local_top = local_top.reshape(samples, 2, head_count)
    fresh_scores = (
        jnp.einsum("athk,ajk->athj", queries, new_rows, preferred_element_type=jnp.float32)
        * score_scale
    )
    steps_seen = jnp.arange(2)[None, None, None, :] <= jnp.arange(2)[None, :, None, None]
    fresh_scores = jnp.where(steps_seen, fresh_scores, floor_score)
    local_top = local_top.at[host_samples].max(jnp.max(fresh_scores, axis=3))
    row_top = lax.pmax(local_top, "seq")
    prompt_top = row_top.reshape(prompts, block_rows)

    def add_page(carry, inputs):
        latent_sums, weight_total = carry
        scores, page_keys, prompt_pick = inputs
        row_best = lax.dynamic_index_in_dim(prompt_top, prompt_pick, 0, keepdims=False)
        weights = jnp.exp(scores - row_best[:, None])
        rounded = weights.astype(jnp.bfloat16)
        page_part = jnp.dot(
            rounded, page_keys[:, :latent_width], preferred_element_type=jnp.float32
        )
        current = lax.dynamic_index_in_dim(latent_sums, prompt_pick, 0, keepdims=True)
        latent_sums = lax.dynamic_update_index_in_dim(
            latent_sums, current + page_part[None], prompt_pick, 0
        )
        current_total = lax.dynamic_index_in_dim(weight_total, prompt_pick, 0, keepdims=True)
        weight_total = lax.dynamic_update_index_in_dim(
            weight_total, current_total + jnp.sum(weights, axis=1)[None], prompt_pick, 0
        )
        return ((latent_sums, weight_total), None)

    empty_sums = (
        jnp.zeros((prompts, block_rows, latent_width), jnp.float32),
        jnp.zeros((prompts, block_rows), jnp.float32),
    )
    (latent_sums, weight_total), _ = lax.scan(
        add_page, empty_sums, (all_scores, cache_pool, page_prompt)
    )
    latent_sums = latent_sums.reshape(samples, 2, head_count, latent_width)
    weight_total = weight_total.reshape(samples, 2, head_count)[all_samples]
    fresh_top = row_top[host_samples]
    fresh_weights = jnp.exp(fresh_scores - fresh_top[..., None])
    fresh_sums = jnp.einsum(
        "athj,ajl->athl",
        fresh_weights.astype(jnp.bfloat16),
        new_rows[..., :latent_width],
        preferred_element_type=jnp.float32,
    )
    fresh_total = jnp.sum(fresh_weights, axis=3)
    up_weight = value_up.astype(jnp.float32)
    summed, total_host = (
        lax.psum_scatter(latent_sums[all_samples], "seq", scatter_dimension=0, tiled=True),
        lax.psum_scatter(weight_total, "seq", scatter_dimension=0, tiled=True),
    )
    latent_out = (summed + fresh_sums) / (total_host + fresh_total)[..., None]
    attended = jnp.einsum("athl,hlv->athv", latent_out, up_weight, precision=lax.Precision.HIGHEST)
    return (new_rows, attended.astype(jnp.bfloat16))


def solution(mesh):
    in_specs = (
        P(("groups", "seq"), None, None),
        P("groups", None),
        P("groups"),
        P(("groups", "seq")),
        P(("groups", "seq"), None, "head", None),
        P(("groups", "seq"), None, "head"),
        P("head", None),
        P(),
        P("head", None, None),
    )
    out_specs = (P(("groups", "seq"), None, None), P(("groups", "seq"), None, "head", None))
    return jax.shard_map(
        on_device, mesh=mesh, in_specs=in_specs, out_specs=out_specs, check_vma=False
    )
```

profile of v0, /device:TPU:0, one launch (start us, length us, event | category | flops | bytes accessed | tf_op | source)
XLA Modules:
  0.0 738.6 jit_solution(14272134272484738927)
XLA Ops:
  10.9 13.2 %all-reduce = s32[16]{0:T(128)S(1)} all-reduce(s32[16]{0:T(128)S(1)} %dynamic-update-slice), channel_id=1, replica_groups=mesh['groups'=2,'seq'=8,'head'=2] {'seq'}, use_global_device_ids=true, to_apply=%add | all-reduce | flops 16 | bytes 128
  24.2 3.4 fusion.19
  27.6 3.3 psum.7
  31.9 23.1 %all-gather.2.cloned.1.call-done = bf16[16,2,32,576]{3,2,1,0:T(8,128)(2,1)} async-done(((bf16[2,2,32,576]{3,2,1,0:T(8,128)(2,1)}), bf16[16,2,32,576]{3,2,1,0:T(8,128)(2,1)}) %all-gather.2.cloned.1.call-update) | async-done | bytes 1179664 | tf_op jit(solution)/shard_map/all_gather | solution.py:44
  55.0 2.1 gather_fusion
  57.1 270.2 %while.22 = (s32[]{:T(128)}, f32[48,512,128]{2,1,0:T(8,128)}, s32[48]{0:T(128)S(1)}, s32[48]{0:T(128)S(1)}, bf16[2,512,576]{2,1,0:T(8,128)(2,1)S(1)}, /*index=5*...) while((s32[]{:T(128)}, f32[48,512,128]{2,1,0:T(8,128)}, s32[48]{0:T(128)S(1)}, ...), condition=%wide.region_8.9_spmd, body=%wide.region_7.8_spmd.sunk | while | flops 75628672 | bytes 1066783 | solution.py:74
  72.1 2.0 fusion.53
  77.7 2.0 fusion.53
  83.3 2.0 fusion.53
  88.9 2.0 fusion.53
  100.2 2.0 fusion.53
  105.8 2.0 fusion.53
  122.7 2.0 fusion.53
  128.4 2.0 fusion.53
  134.0 2.0 fusion.53
  145.3 2.0 fusion.53
  162.1 2.0 fusion.53
  167.8 2.0 fusion.53
  173.4 2.0 fusion.53
  179.0 2.0 fusion.53
  184.7 2.0 fusion.53
  190.3 2.0 fusion.53
  195.9 2.0 fusion.53
  201.6 2.0 fusion.53
  207.2 2.0 fusion.53
  212.8 2.0 fusion.53
  218.4 2.0 fusion.53
  235.3 2.0 fusion.53
  240.9 2.0 fusion.53
  246.6 2.0 fusion.53
  252.2 2.0 fusion.53
  257.8 2.0 fusion.53
  263.5 2.0 fusion.53
  269.1 2.0 fusion.53
  274.7 2.0 fusion.53
  280.4 2.0 fusion.53
  286.0 2.0 fusion.53
  291.7 2.0 fusion.53
  297.3 2.0 fusion.53
  308.5 2.0 fusion.53
  325.4 2.0 fusion.53
  327.4 7.9 %reduce_max.27 = f32[48,512]{1,0:T(8,128)S(1)} reduce(f32[48,512,128]{2,1,0:T(8,128)} %get-tuple-element.226, f32[]{:T(128)} %constant.61.clone.1), dimensions={2}, to_apply=%region_9.10 | reduce | flops 3121152 | bytes 12681220 | tf_op jit(solution)/shard_map/reduce_max | solution.py:75
  336.1 34.8 %pmax.7 = f32[16,2,32]{2,1,0:T(2,128)S(1)} all-reduce(f32[16,2,32]{2,1,0:T(2,128)S(1)} %scatter_fusion), channel_id=1, replica_groups=mesh['groups'=2,'seq'=8,'head'=2] {'seq'}, use_global_device_ids=true, to_apply=%region_13.14 | all-reduce | flops 1024 | bytes 8192 | tf_op jit(solution)/shard_map/pmax | solution.py:87
  371.3 286.8 %while.23 = (s32[]{:T(128)}, f32[2,512,512]{2,1,0:T(8,128)S(1)}, f32[2,512]{1,0:T(2,128)S(1)}, s32[48]{0:T(128)S(1)}, f32[48,512,128]{2,1,0:T(8,128)}, /*index=5...) while((s32[]{:T(128)}, f32[2,512,512]{2,1,0:T(8,128)S(1)}, ...), condition=%wide.region_16.17_spmd, body=%wide.region_14.16_spmd.sunk | while | flops 67633152 | bytes 3068587 | solution.py:113
  658.1 2.0 gather_fusion.1
  662.0 33.3 %all-reduce.1 = f32[16,2,32]{2,1,0:T(2,128)S(1)} all-reduce(f32[16,2,32]{2,1,0:T(2,128)S(1)} %gather_fusion.3), channel_id=3, replica_groups=mesh['groups'=2,'seq'=8,'head'=2] {'seq'}, use_global_device_ids=true, to_apply=%region_18.19.clone | all-reduce | flops 1024 | bytes 8192
  695.3 30.3 %reduce-scatter.2.cloned.1.call-done = f32[2,2,32,512]{3,2,1,0:T(8,128)} async-done(((f32[16,2,32,512]{3,2,1,0:T(8,128)}), f32[2,2,32,512]{3,2,1,0:T(8,128)}) %reduce-scatter.2.cloned.1.call-update) | async-done | bytes 262160 | tf_op jit(solution)/shard_map/reduce_scatter | solution.py:129
  726.9 4.2 fusion.25
  (548 shorter events, 319.6 us)
Async XLA Ops:
  7.2 17.0 %copy-start = (bf16[2,2,3584]{2,1,0:T(2,128)(2,1)S(1)}, bf16[2,2,3584]{2,1,0:T(2,128)(2,1)}, u32[]{:S(2)}) copy-start(bf16[2,2,3584]{2,1,0:T(2,128)(2,1)} %param.18) | copy-start | bytes 86020
  7.2 24.4 %copy-start.6 = (s32[2]{0:T(128)S(1)}, s32[2]{0:T(128)}, u32[]{:S(2)}) copy-start(s32[2]{0:T(128)} %param.16) | copy-start | bytes 28
  7.2 23.8 %copy-start.4 = (f32[512]{0:T(512)S(1)}, f32[512]{0:T(512)}, u32[]{:S(2)}) copy-start(f32[512]{0:T(512)} %param.20) | copy-start | bytes 6148
  7.2 23.9 %copy-start.3 = (s32[2,128]{1,0:T(2,128)S(1)}, s32[2,128]{1,0:T(2,128)}, u32[]{:S(2)}) copy-start(s32[2,128]{1,0:T(2,128)} %param.14) | copy-start | bytes 3076
  7.2 24.1 %copy-start.5 = (s32[2]{0:T(128)S(1)}, s32[2]{0:T(128)}, u32[]{:S(2)}) copy-start(s32[2]{0:T(128)} %param.15) | copy-start | bytes 28
  7.2 47.8 %all-gather.2.cloned.1.call-start = ((), (), s32[]{:S(2)}) async-start(), calls=%async_computation.1 | async-start | bytes 1474560 | tf_op jit(solution)/shard_map/all_gather | solution.py:44
  8.0 23.7 %copy-start.1 = (bf16[2,2,32,576]{3,2,1,0:T(8,128)(2,1)S(1)}, bf16[2,2,32,576]{3,2,1,0:T(8,128)(2,1)}, u32[]{:S(2)}) copy-start(bf16[2,2,32,576]{3,2,1,0:T(8,128)(2,1)} %param.17) | copy-start | bytes 442372
  8.0 717.7 %reduce-scatter.2.cloned.1.call-start = ((), (), s32[]{:S(2)}) async-start(), calls=%async_computation.2 | async-start | bytes 2359296 | tf_op jit(solution)/shard_map/reduce_scatter | solution.py:129
  31.1 26.0 %copy-start.2 = (bf16[2,2,576]{2,1,0:T(2,128)(2,1)}, bf16[2,2,576]{2,1,0:T(2,128)(2,1)S(1)}, u32[]{:S(2)}) copy-start(bf16[2,2,576]{2,1,0:T(2,128)(2,1)S(1)} %pad_maximum_fusion) | copy-start | bytes 13828
Sparse Core Ops, SparseCore 0:
  10.2 44.7 all-gather.1
  660.3 65.3 reduce-scatter.1
where the time goes:
time: 747 us; the launch traced here: 739 us
  loops' own time  177 us (24%)
  matrix products  167 us (22%)
  local copies, waits for them, and re-layouts  144 us (19%)
  other arithmetic  96.3 us (13%)
  blocking collectives  84.6 us (11%)
  waiting for transfers between devices  54.1 us (7%)
  between operations  15.6 us (2%)
    dot_general x48, matrix products, score_page(): lax.dot_general(query_block, page_keys, (((1,), (1,)), ((), ())), preferr...  94.5 us
    another operation x1, loops' own time, on_device(): lax.scan(add_page, empty_sums, (all_scores, cache_pool, page_prompt))  89 us
    dynamic_slice x144, local copies, waits for them, and re-layouts, on_device(): lax.scan(score_page, 0, (cache_pool, page_prompt, live_rows))  88.4 us
    another operation x1, loops' own time, on_device(): lax.scan(score_page, 0, (cache_pool, page_prompt, live_rows))  87.7 us
    dot_general x48, matrix products, add_page(): jnp.dot(rounded, page_keys[:, :latent_width], preferred_element_type=jnp....  63.7 us
    reduce_sum x48, other arithmetic, add_page(): jnp.sum(weights, axis=1)[None]  57.1 us
    unnamed x2, blocking collectives  46.5 us
    squeeze x48, local copies, waits for them, and re-layouts, on_device(): lax.scan(score_page, 0, (cache_pool, page_prompt, live_rows))  44.5 us
  transfers between devices with their start and end apart: 2, of which 2 were waited for; matrix products, arithmetic and copies ran while one was open for 1% of the time, Pallas kernels for 0%

commit v1 on v0

v1 whole, which is shorter than its diff:
```python
import functools

import jax
import jax.numpy as jnp
from jax import lax
from jax.experimental import pallas as pl
from jax.experimental.pallas import tpu as pltpu
from jax.sharding import PartitionSpec as P

eps = 1e-06
log2_scale = 192.0 ** (-0.5) * 1.4426950408889634
floor_score = -1e30
block_pages = 4
fork_count = 8
mesh_ids = pl.DeviceIdType.MESH
vmem = pl.BlockSpec(memory_space=pltpu.VMEM)
smem = pl.BlockSpec(memory_space=pltpu.SMEM)
anywhere = pl.BlockSpec(memory_space=pl.ANY)
trans_b = (((1,), (1,)), ((), ()))


def gather_kernel(
    n, q_ref, hs_ref, nh_ref, down_ref, gain_ref, qall_ref, hsall_ref, rows_ref,
    down_buf, raw_mine, raw_other, down_sem, own_sem, q_send, q_recv, hs_send, hs_recv,
    raw_send, raw_recv,
):
    minor = 2
    major = n // minor
    me = lax.axis_index("seq")
    a, b = me // minor, me % minor
    head = lax.axis_index("head")
    down_copy = pltpu.make_async_copy(down_ref, down_buf, down_sem)
    down_copy.start()
    barrier = pltpu.get_barrier_semaphore()

    def greet(where):
        pl.semaphore_signal(barrier, inc=1, device_id=where, device_id_type=mesh_ids)

    @pl.when(a > 0)
    def _():
        greet({"seq": me - minor})

    @pl.when(a < major - 1)
    def _():
        greet({"seq": me + minor})

    mate = a * minor + (1 - b)
    greet({"seq": mate})
    greet({"head": 1 - head})
    near = jnp.where(a > 0, 1, 0) + jnp.where(a < major - 1, 1, 0)
    pl.semaphore_wait(barrier, 2 + near)

    def copies(src, first, way, dest):
        return (
            pltpu.make_async_remote_copy(
                src_ref=q_ref if first else qall_ref.at[src],
                dst_ref=qall_ref.at[src],
                send_sem=q_send.at[src, way],
                recv_sem=q_recv.at[src],
                device_id={"seq": dest},
                device_id_type=mesh_ids,
            ),
            pltpu.make_async_remote_copy(
                src_ref=hs_ref if first else hsall_ref.at[src],
                dst_ref=hsall_ref.at[src],
                send_sem=hs_send.at[src, way],
                recv_sem=hs_recv.at[src],
                device_id={"seq": dest},
                device_id_type=mesh_ids,
            ),
        )

    def send(src, first, way, dest):
        for copy in copies(src, first, way, dest):
            copy.start()

    def await_send(src, first, way, dest):
        for copy in copies(src, first, way, dest):
            copy.wait_send()

    def await_recv(src):
        for copy in copies(src, False, 0, me):
            copy.wait_recv()

    @pl.when(a > 0)
    def _():
        send(me, True, 0, me - minor)

    @pl.when(a < major - 1)
    def _():
        send(me, True, 1, me + minor)

    send(me, True, 2, mate)
    own_q = pltpu.make_async_copy(q_ref, qall_ref.at[me], own_sem.at[0])
    own_hs = pltpu.make_async_copy(hs_ref, hsall_ref.at[me], own_sem.at[1])
    own_q.start()
    own_hs.start()
    down_copy.wait()
    raw_mine[...] = lax.dot_general(
        nh_ref[...], down_buf[...], trans_b, preferred_element_type=jnp.float32
    )[0:8]
    raw_copy = pltpu.make_async_remote_copy(
        src_ref=raw_mine,
        dst_ref=raw_other,
        send_sem=raw_send,
        recv_sem=raw_recv,
        device_id={"head": 1 - head},
        device_id_type=mesh_ids,
    )
    raw_copy.start()

    def forward_down(d):
        src = me + d * minor

        @pl.when(a + d < major)
        def _():
            await_recv(src)

            @pl.when(a > 0)
            def _():
                send(src, False, 0, me - minor)

            send(src, False, 2, mate)

    def forward_up(d):
        src = me - d * minor

        @pl.when(a - d >= 0)
        def _():
            await_recv(src)

            @pl.when(a < major - 1)
            def _():
                send(src, False, 1, me + minor)

            send(src, False, 2, mate)

    for d in range(1, major):
        forward_down(d)
        forward_up(d)
        if d == 1:
            raw_copy.wait()
            raw = raw_mine[...] + raw_other[...]
            width = gain_ref.shape[1]
            latent = raw[:, :width]
            spread = lax.rsqrt(jnp.mean(latent * latent, axis=-1, keepdims=True) + eps)
            rows_ref[0:8, :width] = (latent * spread * gain_ref[...]).astype(jnp.bfloat16)
            rows_ref[0:8, width:] = raw[:, width:].astype(jnp.bfloat16)
            rows_ref[8:16, :] = jnp.zeros((8, raw.shape[1]), jnp.bfloat16)
    for c in range(major):
        await_recv(c * minor + (1 - b))
    own_q.wait()
    own_hs.wait()

    for c in range(major):
        src = c * minor + b

        @pl.when(jnp.logical_and(a > 0, c >= a))
        def _():
            await_send(src, False, 0, me - minor)

        @pl.when(jnp.logical_and(a < major - 1, c <= a))
        def _():
            await_send(src, False, 1, me + minor)

        await_send(src, False, 2, mate)


def attend_kernel(
    list_ref, live_ref, count_ref, hs_ref, q_ref, fresh_ref, pool_ref, up_ref, o_ref, ml_ref,
    kbuf, sbuf, sfresh, qp, acc, oacc, mbuf, lbuf, mlcol, upbuf, slot_of, page_sem, up_sem,
):
    prompts = list_ref.shape[0]
    per_host = 2
    slots, slot_rows, width = q_ref.shape
    heads, latent, vhead = up_ref.shape
    rows = fork_count * slot_rows
    me = lax.axis_index("seq")

    def page_copy(p, i, at):
        return pltpu.make_async_copy(pool_ref.at[list_ref[p, i]], kbuf.at[at], page_sem.at[at])

    def blocks_of(p):
        return (count_ref[p] + block_pages - 1) // block_pages

    def start_prompt(p, base):
        count = blocks_of(p) * block_pages

        def start_page(i, carry):
            page_copy(p, i, base + i).start()
            return carry

        lax.fori_loop(0, count, start_page, 0)
        return base + count

    lax.fori_loop(0, prompts, start_prompt, 0)
    up_copy = pltpu.make_async_copy(up_ref, upbuf, up_sem)
    up_copy.start()

    def note_slot(i, carry):
        slot_of[hs_ref[i // per_host, 0, i % per_host]] = i
        return carry

    lax.fori_loop(0, slots, note_slot, 0)
    lane = lax.broadcasted_iota(jnp.int32, (1, 128), 1)
    fresh_lane = lax.broadcasted_iota(jnp.int32, (slot_rows, 16), 1)
    step_of = lax.broadcasted_iota(jnp.int32, (slot_rows, 16), 0) // heads
    step_ok = jnp.logical_and(fresh_lane % 2 <= step_of, fresh_lane < 2 * per_host)

    def one_prompt(p, base):
        for f in range(fork_count):
            qp[f * slot_rows : (f + 1) * slot_rows, :] = q_ref[slot_of[p * fork_count + f]]
        fresh_all = (
            lax.dot_general(qp[...], fresh_ref[...], trans_b, preferred_element_type=jnp.float32)
            * log2_scale
        )
        for f in range(fork_count):
            part = slice(f * slot_rows, (f + 1) * slot_rows)
            mine = slot_of[p * fork_count + f] - me * per_host
            seen = jnp.logical_and(step_ok, fresh_lane // 2 == mine)
            scores = jnp.where(seen, fresh_all[part], floor_score)
            sfresh[part, :] = scores
            mbuf[part, :] = jnp.broadcast_to(
                jnp.max(scores, axis=1, keepdims=True), (slot_rows, 128)
            )
        blocks = blocks_of(p)

        def score_block(j, carry):
            for i in range(block_pages):
                page_copy(p, j * block_pages + i, base + j * block_pages + i).wait()
            keys = jnp.concatenate(
                [kbuf[base + j * block_pages + i] for i in range(block_pages)], axis=1
            )
            scores = jnp.dot(qp[...], keys, preferred_element_type=jnp.float32) * log2_scale
            top = mbuf[...]
            for i in range(block_pages):
                live = live_ref[p, j * block_pages + i]
                piece = jnp.where(lane < live, scores[:, i * 128 : (i + 1) * 128], floor_score)
                sbuf[j, :, i * 128 : (i + 1) * 128] = piece
                top = jnp.maximum(top, piece)
            mbuf[...] = top
            return carry

        lax.fori_loop(0, blocks, score_block, 0)
        top = jnp.max(mbuf[...], axis=1, keepdims=True)
        mbuf[...] = jnp.broadcast_to(top, (rows, 128))
        fresh_scores = sfresh[...]
        fresh_w = jnp.where(fresh_scores > floor_score, jnp.exp2(fresh_scores - top), 0.0)
        fresh_total = jnp.sum(fresh_w, axis=1, keepdims=True)
        lbuf[...] = jnp.where(lane == 0, fresh_total, 0.0)
        fresh_w = fresh_w.astype(jnp.bfloat16)
        for c in range(latent // 128):
            acc[c] = jnp.dot(
                fresh_w, fresh_ref[:, c * 128 : (c + 1) * 128], preferred_element_type=jnp.float32
            )

        def add_block(j, carry):
            keys = jnp.concatenate(
                [kbuf[base + j * block_pages + i, :latent] for i in range(block_pages)], axis=1
            )
            top = mbuf[...]
            total = lbuf[...]
            rounded = []
            for i in range(block_pages):
                w = jnp.exp2(sbuf[j, :, i * 128 : (i + 1) * 128] - top)
                total = total + w
                rounded.append(w.astype(jnp.bfloat16))
            lbuf[...] = total
            part = lax.dot_general(
                jnp.concatenate(rounded, axis=1), keys, trans_b,
                preferred_element_type=jnp.float32,
            )
            for c in range(latent // 128):
                acc[c] += part[:, c * 128 : (c + 1) * 128]
            return carry

        lax.fori_loop(0, blocks, add_block, 0)
        total = jnp.sum(lbuf[...], axis=1, keepdims=True)
        ml = jnp.where(lane == 0, mbuf[...], total)

        @pl.when(p == 0)
        def _():
            up_copy.wait()

        group = 2 * fork_count
        for h in range(heads):
            x = jnp.concatenate(
                [acc[c, pl.ds(h, group, stride=heads), :] for c in range(latent // 128)], axis=1
            )
            hi = x.astype(jnp.bfloat16)
            lo = (x - hi.astype(jnp.float32)).astype(jnp.bfloat16)
            y = jnp.dot(
                jnp.concatenate([hi, lo], axis=0), upbuf[h], preferred_element_type=jnp.float32
            )
            oacc[pl.ds(h, group, stride=heads), :] = y[:group] + y[group:]
        for f in range(fork_count):
            part = slice(f * slot_rows, (f + 1) * slot_rows)
            slot = slot_of[p * fork_count + f]
            o_ref[slot] = oacc[part, :]
            mlcol[slot] = ml[part]
        return base + blocks * block_pages

    lax.fori_loop(0, prompts, one_prompt, 0)

    def turn(d, carry):
        both = mlcol[pl.ds(d * per_host, per_host)].reshape(per_host * slot_rows, 128)
        ml_ref[d] = both.T[0:8]
        return carry

    lax.fori_loop(0, slots // per_host, turn, 0)


def combine_kernel(
    n, o_ref, ml_ref, out_ref, o_got, ml_got, gains, o_send, o_recv, ml_send, ml_recv
):
    me = lax.axis_index("seq")
    barrier = pltpu.get_barrier_semaphore()
    for k in range(1, n):
        pl.semaphore_signal(
            barrier, inc=1, device_id={"seq": (me + k) % n}, device_id_type=mesh_ids
        )
    pl.semaphore_wait(barrier, n - 1)
    copies = []
    for k in range(1, n):
        dest = (me + k) % n
        for src, got, s_sem, r_sem in (
            (ml_ref, ml_got, ml_send, ml_recv),
            (o_ref, o_got, o_send, o_recv),
        ):
            copy = pltpu.make_async_remote_copy(
                src_ref=src.at[dest],
                dst_ref=got.at[k],
                send_sem=s_sem.at[k],
                recv_sem=r_sem.at[k],
                device_id={"seq": dest},
                device_id_type=mesh_ids,
            )
            copy.start()
            copies.append(copy)
    ml_got[0] = ml_ref[me]
    o_got[0] = o_ref[me]
    for copy in copies:
        copy.wait()
    top = ml_got[0, 0:1, :]
    for k in range(1, n):
        top = jnp.maximum(top, ml_got[k, 0:1, :])
    total = jnp.zeros_like(top)
    gains[...] = jnp.zeros_like(gains)
    for k in range(n):
        factor = jnp.exp2(ml_got[k, 0:1, :] - top)
        gains[k : k + 1, :] = factor
        total = total + factor * ml_got[k, 1:2, :]
    turned = (gains[...] / total).T
    out = turned[:, 0:1] * o_got[0]
    for k in range(1, n):
        out = out + turned[:, k : k + 1] * o_got[k]
    out_ref[...] = out.astype(jnp.bfloat16)


def on_device(
    cache_pool, page_table, prompt_len, host_samples, queries, new_hidden, kv_down, kv_gain,
    value_up,
):
    n = lax.axis_size("seq")
    me = lax.axis_index("seq")
    per_host, steps, heads, width = queries.shape
    latent = kv_gain.shape[0]
    vhead = value_up.shape[2]
    page_count, page_rows = cache_pool.shape[:2]
    prompts, table_width = page_table.shape
    host_rows = per_host * steps * heads
    slot_rows = steps * heads
    slots = n * per_host
    rows = fork_count * slot_rows
    local = page_table - me * page_count
    owned = jnp.logical_and(local >= 0, local < page_count)
    column = jnp.arange(table_width, dtype=jnp.int32)
    before = column[None, :] < column[:, None]
    rank = jnp.sum(
        jnp.where(jnp.logical_and(before[None], owned[:, None, :]), 1, 0), axis=2, dtype=jnp.int32
    )
    list_width = -(-page_count // block_pages) * block_pages
    order = jnp.arange(list_width, dtype=jnp.int32)
    hot = jnp.logical_and(owned[:, None, :], rank[:, None, :] == order[None, :, None])
    page_list = jnp.sum(jnp.where(hot, local[:, None, :], 0), axis=2, dtype=jnp.int32)
    left = jnp.minimum(prompt_len[:, None] - column[None, :] * page_rows, page_rows)
    page_live = jnp.sum(jnp.where(hot, left[:, None, :], 0), axis=2, dtype=jnp.int32)
    counts = jnp.sum(owned, axis=1, dtype=jnp.int32)

    hs_tile = jnp.pad(host_samples[None, :], ((0, 7), (0, 128 - per_host)))
    hidden = jnp.pad(
        new_hidden.reshape(per_host * steps, -1), ((0, 16 - per_host * steps), (0, 0))
    )
    big = pltpu.CompilerParams
    qall, hsall, rows16 = pl.pallas_call(
        functools.partial(gather_kernel, n),
        out_shape=(
            jax.ShapeDtypeStruct((n, host_rows, width), jnp.bfloat16),
            jax.ShapeDtypeStruct((n, 8, 128), jnp.int32),
            jax.ShapeDtypeStruct((16, width), jnp.bfloat16),
        ),
        in_specs=[vmem, vmem, vmem, anywhere, vmem],
        out_specs=(vmem, vmem, vmem),
        scratch_shapes=[
            pltpu.VMEM(kv_down.shape[::-1], jnp.bfloat16),
            pltpu.VMEM((8, width), jnp.float32),
            pltpu.VMEM((8, width), jnp.float32),
            pltpu.SemaphoreType.DMA,
            pltpu.SemaphoreType.DMA((2,)),
            pltpu.SemaphoreType.DMA((n, 3)),
            pltpu.SemaphoreType.DMA((n,)),
            pltpu.SemaphoreType.DMA((n, 3)),
            pltpu.SemaphoreType.DMA((n,)),
            pltpu.SemaphoreType.DMA,
            pltpu.SemaphoreType.DMA,
        ],
        compiler_params=big(
            collective_id=0, has_side_effects=True, vmem_limit_bytes=48 * 2**20
        ),
    )(queries.reshape(host_rows, width), hs_tile, hidden, kv_down.T, kv_gain[None, :])
    new_rows = rows16[: per_host * steps].reshape(per_host, steps, width)

    slots_held = -(-page_count // block_pages) * block_pages + (block_pages - 1) * prompts
    o, ml = pl.pallas_call(
        attend_kernel,
        out_shape=(
            jax.ShapeDtypeStruct((slots, slot_rows, vhead), jnp.float32),
            jax.ShapeDtypeStruct((n, 8, 128), jnp.float32),
        ),
        in_specs=[smem, smem, smem, smem, vmem, vmem, anywhere, anywhere],
        out_specs=(vmem, vmem),
        scratch_shapes=[
            pltpu.VMEM((slots_held, width, page_rows), jnp.bfloat16),
            pltpu.VMEM((list_width // block_pages, rows, block_pages * page_rows), jnp.float32),
            pltpu.VMEM((rows, 16), jnp.float32),
            pltpu.VMEM((rows, width), jnp.bfloat16),
            pltpu.VMEM((latent // 128, rows, 128), jnp.float32),
            pltpu.VMEM((rows, vhead), jnp.float32),
            pltpu.VMEM((rows, 128), jnp.float32),
            pltpu.VMEM((rows, 128), jnp.float32),
            pltpu.VMEM((slots, slot_rows, 128), jnp.float32),
            pltpu.VMEM(value_up.shape, jnp.bfloat16),
            pltpu.SMEM((slots,), jnp.int32),
            pltpu.SemaphoreType.DMA((slots_held,)),
            pltpu.SemaphoreType.DMA,
        ],
        compiler_params=big(vmem_limit_bytes=60 * 2**20),
    )(
        page_list, page_live, counts, hsall, qall.reshape(slots, slot_rows, width), rows16,
        jnp.swapaxes(cache_pool, 1, 2), value_up,
    )

    out = pl.pallas_call(
        functools.partial(combine_kernel, n),
        out_shape=jax.ShapeDtypeStruct((host_rows, vhead), jnp.bfloat16),
        in_specs=[vmem, vmem],
        out_specs=vmem,
        scratch_shapes=[
            pltpu.VMEM((n, host_rows, vhead), jnp.float32),
            pltpu.VMEM((n, 8, 128), jnp.float32),
            pltpu.VMEM((128, 128), jnp.float32),
            pltpu.SemaphoreType.DMA((n,)),
            pltpu.SemaphoreType.DMA((n,)),
            pltpu.SemaphoreType.DMA((n,)),
            pltpu.SemaphoreType.DMA((n,)),
        ],
        compiler_params=big(
            collective_id=1, has_side_effects=True, vmem_limit_bytes=48 * 2**20
        ),
    )(o.reshape(n, host_rows, vhead), ml)
    return (new_rows, out.reshape(per_host, steps, heads, vhead))


def solution(mesh):
    in_specs = (
        P(("groups", "seq"), None, None),
        P("groups", None),
        P("groups"),
        P(("groups", "seq")),
        P(("groups", "seq"), None, "head", None),
        P(("groups", "seq"), None, "head"),
        P("head", None),
        P(),
        P("head", None, None),
    )
    out_specs = (P(("groups", "seq"), None, None), P(("groups", "seq"), None, "head", None))
    return jax.shard_map(
        on_device, mesh=mesh, in_specs=in_specs, out_specs=out_specs, check_vma=False
    )
```

time: 747 us -> 68.6 us (0.09)
  the two profiles are of different devices: /device:TPU:0 before, /device:TPU:14 now
where the time goes in v1:
time: 68.6 us; the launch traced here: 68 us
  Pallas kernels  53.8 us (78%)
  local copies, waits for them, and re-layouts  11.2 us (16%)
  other arithmetic  2.27 us (3%)
  between operations  0.7 us (1%)
    pallas_call x1, Pallas kernels, on_device(): pl.pallas_call(functools.partial(gather_kernel, n), out_shape=(jax.ShapeD...  19.5 us
    pallas_call x1, Pallas kernels, on_device(): pl.pallas_call(functools.partial(combine_kernel, n), out_shape=jax.ShapeD...  17.8 us
    pallas_call x1, Pallas kernels, on_device(): pl.pallas_call(attend_kernel, out_shape=(jax.ShapeDtypeStruct((slots, slo...  16.5 us
    unnamed x17, local copies, waits for them, and re-layouts  8.46 us
    reduce_sum x1, other arithmetic, on_device(): counts = jnp.sum(owned, axis=1, dtype=jnp.int32)  1.38 us

profile of v1, /device:TPU:14, one launch (start us, length us, event | category | flops | bytes accessed | tf_op | source)
XLA Modules:
  0.0 68.0 jit_solution(3463646963594104451)
XLA Ops:
  0.6 1.4 %convert_reduce_fusion = (s32[2]{0:T(128)}, pred[2,128]{1,0:T(4,128)(4,1)S(1)}, s32[2,128]{1,0:T(2,128)S(1)}, s32[2,128]{1,0:T(2,128)S(1)}) fusion(s32[2,128]{1,0:T(2,128)} %param.10, s32[]{:T(128)S(6)} %mul.14, s32[128]{0:T(128)S(1)} %iota_multiply_fusion, s32[2]{0:T(128)} %param.11), kind=kLoop, calls=%fused_computation.7 | loop fusion | flops 2046 | bytes 3860 | tf_op jit(solution)/shard_map/reduce_sum | solution.py:388
  2.0 0.7 pad.8.hs_ref
  2.7 0.1 select_reduce_fusion
  2.8 0.7 %select_reduce_fusion.1 = (s32[2,48]{1,0:T(2,128)}, s32[2,48]{1,0:T(2,128)}) fusion(s32[2,128]{1,0:T(2,128)S(1)} %get-tuple-element.17, s32[2,128]{1,0:T(2,128)S(1)} %select_reduce_fusion, pred[2,128]{1,0:T(4,128)(4,1)S(1)} %get-tuple-element.15, s32[2,128]{1,0:T(2,128)S(1)} %get-tuple-element.16), kind=kLoop, calls=%fused_computation.2 | loop fusion | flops 73536 | bytes 4096 | tf_op jit(solution)/shard_map/reduce_sum | solution.py:387
  3.6 0.8 %reshape.67 = bf16[4,3584]{1,0:T(4,128)(2,1)S(1)} reshape(bf16[2,2,3584]{2,1,0:T(2,128)(2,1)} %param.14) | data formatting | bytes 57344 | tf_op jit(solution)/shard_map/reshape | solution.py:392
  4.4 0.0 copy-start
  4.4 2.2 %copy-done = bf16[3584,576]{0,1:T(8,128)(2,1)S(1)} copy-done((bf16[3584,576]{0,1:T(8,128)(2,1)S(1)}, bf16[3584,576]{0,1:T(8,128)(2,1)}, u32[]{:S(2)}) %copy-start) | copy-done | bytes 4128792
  6.5 0.0 copy-start.3
  6.5 0.9 %copy-done.3 = bf16[2,2,32,576]{3,2,1,0:T(8,128)(2,1)S(1)} copy-done((bf16[2,2,32,576]{3,2,1,0:T(8,128)(2,1)S(1)}, bf16[2,2,32,576]{3,2,1,0:T(8,128)(2,1)}, u32[]{:S(2)}) %copy-start.3) | copy-done | bytes 147480
  7.4 0.0 copy-start.7
  7.4 0.7 copy-done.7
  8.1 19.5 %shard_map.104 = (bf16[8,128,576]{2,1,0:T(8,128)(2,1)S(1)}, s32[8,8,128]{2,1,0:T(8,128)S(1)}, bf16[16,576]{1,0:T(8,128)(2,1)S(1)}) custom-call(bf16[128,576]{1,0:T(8,128)(2,1)S(1)} %bitcast.11, s32[8,128]{1,0:T(8,128)S(1)} %pad.8.hs_ref, bf16[16,3584]{1,0:T(8,128)(2,1)S(1)} %pad.9.nh_ref, bf16[576,3584]{1,0:T(8,128)(2,1)S(1)} %bitcast.8, f32[1,512]{1,0:T(1,128)S(1)} %bitcast.13), custom_call_target="tpu_custom_call" | custom-call | tf_op jit(solution)/shard_map/pallas_call | solution.py:395
  27.6 0.0 copy-start.1
  27.6 1.1 %copy-done.1 = bf16[8,128,576]{2,1,0:T(8,128)(2,1)} copy-done((bf16[8,128,576]{2,1,0:T(8,128)(2,1)}, bf16[8,128,576]{2,1,0:T(8,128)(2,1)S(1)}, u32[]{:S(2)}) %copy-start.1) | copy-done | bytes 1179672
  28.7 0.0 copy-start.4
  28.7 0.6 copy-done.4
  29.3 0.0 copy-start.6
  29.3 0.6 copy-done.6
  29.9 16.5 %shard_map.105 = (f32[16,64,128]{2,1,0:T(8,128)}, f32[8,8,128]{2,1,0:T(8,128)}) custom-call(s32[2,48]{1,0:T(2,128)} %get-tuple-element.13.list_ref, s32[2,48]{1,0:T(2,128)} %get-tuple-element.12.live_ref, s32[2]{0:T(128)} %get-tuple-element.14.count_ref, s32[8,8,128]{2,1,0:T(8,128)} %copy-done.4, bf16[16,64,576]{2,1,0:T(8,128)(2,1)} %bitcast.9, ...), custom_call_target="tpu_custom_call" | custom-call | tf_op jit(solution)/shard_map/pallas_call | solution.py:424
  46.4 0.7 %slice.3 = bf16[4,576]{1,0:T(4,128)(2,1)S(1)} slice(bf16[16,576]{1,0:T(8,128)(2,1)} %copy-done.6), slice={[0:4], [0:576]} | slice | bytes 9216 | tf_op jit(solution)/shard_map/slice | solution.py:421
  47.1 0.6 reshape.68
  47.8 0.0 copy-start.2
  47.8 1.0 %copy-done.2 = f32[16,64,128]{2,1,0:T(8,128)S(1)} copy-done((f32[16,64,128]{2,1,0:T(8,128)S(1)}, f32[16,64,128]{2,1,0:T(8,128)}, u32[]{:S(2)}) %copy-start.2) | copy-done | bytes 524312
  48.8 0.0 copy-start.5
  48.8 0.8 %copy-done.5 = f32[8,8,128]{2,1,0:T(8,128)S(1)} copy-done((f32[8,8,128]{2,1,0:T(8,128)S(1)}, f32[8,8,128]{2,1,0:T(8,128)}, u32[]{:S(2)}) %copy-start.5) | copy-done | bytes 32792
  49.6 17.8 %shard_map.106 = bf16[128,128]{1,0:T(8,128)(2,1)S(1)} custom-call(f32[8,128,128]{2,1,0:T(8,128)S(1)} %bitcast.10, f32[8,8,128]{2,1,0:T(8,128)S(1)} %copy-done.5), custom_call_target="tpu_custom_call" | custom-call | tf_op jit(solution)/shard_map/pallas_call | solution.py:453
  67.4 0.6 copy.12
  (3 shorter events, 0.0 us)
Async XLA Ops:
  4.4 2.2 %copy-start = (bf16[3584,576]{0,1:T(8,128)(2,1)S(1)}, bf16[3584,576]{0,1:T(8,128)(2,1)}, u32[]{:S(2)}) copy-start(bf16[3584,576]{0,1:T(8,128)(2,1)} %param.15) | copy-start | bytes 12386308
  6.5 0.9 %copy-start.3 = (bf16[2,2,32,576]{3,2,1,0:T(8,128)(2,1)S(1)}, bf16[2,2,32,576]{3,2,1,0:T(8,128)(2,1)}, u32[]{:S(2)}) copy-start(bf16[2,2,32,576]{3,2,1,0:T(8,128)(2,1)} %param.13) | copy-start | bytes 442372
  7.4 0.7 %copy-start.7 = (f32[512]{0:T(512)S(1)}, f32[512]{0:T(512)}, u32[]{:S(2)}) copy-start(f32[512]{0:T(512)} %param.16) | copy-start | bytes 6148
  27.6 1.1 %copy-start.1 = (bf16[8,128,576]{2,1,0:T(8,128)(2,1)}, bf16[8,128,576]{2,1,0:T(8,128)(2,1)S(1)}, u32[]{:S(2)}) copy-start(bf16[8,128,576]{2,1,0:T(8,128)(2,1)S(1)} %get-tuple-element.9) | copy-start | bytes 3538948
  28.7 0.6 copy-start.4
  29.3 0.6 copy-start.6
  47.8 1.0 %copy-start.2 = (f32[16,64,128]{2,1,0:T(8,128)S(1)}, f32[16,64,128]{2,1,0:T(8,128)}, u32[]{:S(2)}) copy-start(f32[16,64,128]{2,1,0:T(8,128)} %get-tuple-element.10) | copy-start | bytes 1572868
  48.8 0.8 %copy-start.5 = (f32[8,8,128]{2,1,0:T(8,128)S(1)}, f32[8,8,128]{2,1,0:T(8,128)}, u32[]{:S(2)}) copy-start(f32[8,8,128]{2,1,0:T(8,128)} %get-tuple-element.11.ml_ref) | copy-start | bytes 98308

commit v2 on v1

--- a/solution.py
+++ b/solution.py
@@ -15,20 +15,22 @@
 mesh_ids = pl.DeviceIdType.MESH
 vmem = pl.BlockSpec(memory_space=pltpu.VMEM)
 smem = pl.BlockSpec(memory_space=pltpu.SMEM)
-anywhere = pl.BlockSpec(memory_space=pl.ANY)
+hbm = pl.BlockSpec(memory_space=pltpu.HBM)
 trans_b = (((1,), (1,)), ((), ()))
 
 
 def gather_kernel(
-    n, q_ref, hs_ref, nh_ref, down_ref, gain_ref, qall_ref, hsall_ref, rows_ref,
-    down_buf, raw_mine, raw_other, down_sem, own_sem, q_send, q_recv, hs_send, hs_recv,
-    raw_send, raw_recv,
+    n, page_count, page_rows, q_ref, host_ref, nh_ref, down_ref, gain_ref, table_ref, len_ref,
+    qall_ref, hsall_ref, rows_ref, new_ref, list_ref,
+    down_buf, raw_mine, raw_other, nh_buf, hs_ref, rows_buf, list_buf, down_sem, own_sem, q_send,
+    q_recv, hs_send, hs_recv, raw_send, raw_recv,
 ):
     minor = 2
     major = n // minor
     me = lax.axis_index("seq")
     a, b = me // minor, me % minor
     head = lax.axis_index("head")
+    half = q_ref.shape[0] // 2
     down_copy = pltpu.make_async_copy(down_ref, down_buf, down_sem)
     down_copy.start()
     barrier = pltpu.get_barrier_semaphore()
@@ -47,58 +49,76 @@
     mate = a * minor + (1 - b)
     greet({"seq": mate})
     greet({"head": 1 - head})
+    lane = lax.broadcasted_iota(jnp.int32, (8, 128), 1)
+    tile = jnp.zeros((8, 128), jnp.int32)
+    for i in range(host_ref.shape[0]):
+        tile = jnp.where(lane == i, host_ref[i], tile)
+    hs_ref[...] = tile
     near = jnp.where(a > 0, 1, 0) + jnp.where(a < major - 1, 1, 0)
     pl.semaphore_wait(barrier, 2 + near)
 
-    def copies(src, first, way, dest):
-        return (
+    def copies(src, c, first, way, dest):
+        rows = pl.ds(c * half, half)
+        found = [
             pltpu.make_async_remote_copy(
-                src_ref=q_ref if first else qall_ref.at[src],
-                dst_ref=qall_ref.at[src],
-                send_sem=q_send.at[src, way],
-                recv_sem=q_recv.at[src],
+                src_ref=q_ref.at[rows] if first else qall_ref.at[src, rows],
+                dst_ref=qall_ref.at[src, rows],
+                send_sem=q_send.at[src, way, c],
+                recv_sem=q_recv.at[src, c],
                 device_id={"seq": dest},
                 device_id_type=mesh_ids,
-            ),
-            pltpu.make_async_remote_copy(
-                src_ref=hs_ref if first else hsall_ref.at[src],
-                dst_ref=hsall_ref.at[src],
-                send_sem=hs_send.at[src, way],
-                recv_sem=hs_recv.at[src],
-                device_id={"seq": dest},
-                device_id_type=mesh_ids,
-            ),
-        )
-
-    def send(src, first, way, dest):
-        for copy in copies(src, first, way, dest):
+            )
+        ]
+        if c == 0:
+            found.append(
+                pltpu.make_async_remote_copy(
+                    src_ref=hs_ref if first else hsall_ref.at[src],
+                    dst_ref=hsall_ref.at[src],
+                    send_sem=hs_send.at[src, way],
+                    recv_sem=hs_recv.at[src],
+                    device_id={"seq": dest},
+                    device_id_type=mesh_ids,
+                )
+            )
+        return found
+
+    def send(src, c, first, way, dest):
+        for copy in copies(src, c, first, way, dest):
             copy.start()
 
     def await_send(src, first, way, dest):
-        for copy in copies(src, first, way, dest):
-            copy.wait_send()
-
-    def await_recv(src):
-        for copy in copies(src, False, 0, me):
+        for c in range(2):
+            for copy in copies(src, c, first, way, dest):
+                copy.wait_send()
+
+    def await_recv(src, c):
+        for copy in copies(src, c, False, 0, me):
             copy.wait_recv()
 
-    @pl.when(a > 0)
-    def _():
-        send(me, True, 0, me - minor)
-
-    @pl.when(a < major - 1)
-    def _():
-        send(me, True, 1, me + minor)
-
-    send(me, True, 2, mate)
+    for c in range(2):
+
+        @pl.when(a > 0)
+        def _():
+            send(me, c, True, 0, me - minor)
+
+        @pl.when(a < major - 1)
+        def _():
+            send(me, c, True, 1, me + minor)
+
+        send(me, c, True, 2, mate)
     own_q = pltpu.make_async_copy(q_ref, qall_ref.at[me], own_sem.at[0])
     own_hs = pltpu.make_async_copy(hs_ref, hsall_ref.at[me], own_sem.at[1])
     own_q.start()
     own_hs.start()
+    per_host, steps = nh_ref.shape[:2]
+    nh_buf[...] = jnp.zeros_like(nh_buf)
+    for i in range(per_host):
+        nh_buf[i * steps : (i + 1) * steps, :] = nh_ref[i].astype(jnp.float32)
     down_copy.wait()
     raw_mine[...] = lax.dot_general(
-        nh_ref[...], down_buf[...], trans_b, preferred_element_type=jnp.float32
-    )[0:8]
+        nh_buf[...].astype(jnp.bfloat16), down_buf[...], trans_b,
+        preferred_element_type=jnp.float32,
+    )
     raw_copy = pltpu.make_async_remote_copy(
         src_ref=raw_mine,
         dst_ref=raw_other,
@@ -109,57 +129,100 @@
     )
     raw_copy.start()
 
-    def forward_down(d):
+    def forward_down(d, c):
         src = me + d * minor
 
         @pl.when(a + d < major)
         def _():
-            await_recv(src)
+            await_recv(src, c)
 
             @pl.when(a > 0)
             def _():
-                send(src, False, 0, me - minor)
-
-            send(src, False, 2, mate)
-
-    def forward_up(d):
+                send(src, c, False, 0, me - minor)
+
+            send(src, c, False, 2, mate)
+
+    def forward_up(d, c):
         src = me - d * minor
 
         @pl.when(a - d >= 0)
         def _():
-            await_recv(src)
+            await_recv(src, c)
 
             @pl.when(a < major - 1)
             def _():
-                send(src, False, 1, me + minor)
-
-            send(src, False, 2, mate)
-
+                send(src, c, False, 1, me + minor)
+
+            send(src, c, False, 2, mate)
+
+    def page_lists():
+        prompts, table_width = table_ref.shape
+        list_width = list_buf.shape[2]
+        column = lax.broadcasted_iota(jnp.int32, (1, table_width), 1)
+        earlier = lax.broadcasted_iota(jnp.int32, (table_width, table_width), 0)
+        later = lax.broadcasted_iota(jnp.int32, (table_width, table_width), 1)
+        before = jnp.where(earlier < later, 1.0, 0.0).astype(jnp.bfloat16)
+        order = lax.broadcasted_iota(jnp.int32, (list_width, table_width), 0)
+        line = lax.broadcasted_iota(jnp.int32, (8, table_width), 0)
+        for p in range(prompts):
+            local = table_ref[p : p + 1, :] - me * page_count
+            owned = jnp.where(jnp.logical_and(local >= 0, local < page_count), 1, 0)
+            many = jnp.broadcast_to(owned, (8, table_width)).astype(jnp.float32)
+            rank = jnp.dot(
+                many.astype(jnp.bfloat16), before, preferred_element_type=jnp.float32
+            )[0:1].astype(jnp.int32)
+            hot = jnp.where(jnp.logical_and(order == rank, owned > 0), 1.0, 0.0)
+            left = jnp.minimum(len_ref[p] - column * page_rows, page_rows)
+            count = jnp.sum(owned, axis=1, keepdims=True)
+            values = jnp.where(line == 0, local * owned, left * owned).astype(jnp.float32)
+            picked = lax.dot_general(
+                values.astype(jnp.bfloat16), hot.astype(jnp.bfloat16), trans_b,
+                preferred_element_type=jnp.float32,
+            ).astype(jnp.int32)
+            picked_line = lax.broadcasted_iota(jnp.int32, picked.shape, 0)
+            list_buf[p] = jnp.where(picked_line == 2, count, picked)
+
+    width = gain_ref.shape[1]
+    extra = []
     for d in range(1, major):
-        forward_down(d)
-        forward_up(d)
+        for c in range(2):
+            forward_down(d, c)
+            forward_up(d, c)
         if d == 1:
             raw_copy.wait()
             raw = raw_mine[...] + raw_other[...]
-            width = gain_ref.shape[1]
             latent = raw[:, :width]
             spread = lax.rsqrt(jnp.mean(latent * latent, axis=-1, keepdims=True) + eps)
-            rows_ref[0:8, :width] = (latent * spread * gain_ref[...]).astype(jnp.bfloat16)
-            rows_ref[0:8, width:] = raw[:, width:].astype(jnp.bfloat16)
-            rows_ref[8:16, :] = jnp.zeros((8, raw.shape[1]), jnp.bfloat16)
-    for c in range(major):
-        await_recv(c * minor + (1 - b))
+            done = jnp.concatenate(
+                [latent * spread * gain_ref[...], raw[:, width:]], axis=1
+            )
+            rows_buf[...] = jnp.concatenate([done, jnp.zeros_like(done)], axis=0).astype(
+                jnp.bfloat16
+            )
+            for i in range(per_host):
+                new_ref[i] = done[i * steps : (i + 1) * steps].astype(jnp.bfloat16)
+            page_lists()
+            extra = [
+                pltpu.make_async_copy(rows_buf, rows_ref, own_sem.at[2]),
+                pltpu.make_async_copy(list_buf, list_ref, own_sem.at[3]),
+            ]
+            for copy in extra:
+                copy.start()
+    for k in range(major):
+        for c in range(2):
+            await_recv(k * minor + (1 - b), c)
     own_q.wait()
     own_hs.wait()
-
-    for c in range(major):
-        src = c * minor + b
-
-        @pl.when(jnp.logical_and(a > 0, c >= a))
+    for copy in extra:
+        copy.wait()
+    for k in range(major):
+        src = k * minor + b
+
+        @pl.when(jnp.logical_and(a > 0, k >= a))
         def _():
             await_send(src, False, 0, me - minor)
 
-        @pl.when(jnp.logical_and(a < major - 1, c <= a))
+        @pl.when(jnp.logical_and(a < major - 1, k <= a))
         def _():
             await_send(src, False, 1, me + minor)
 
@@ -167,7 +230,7 @@
 
 
 def attend_kernel(
-    list_ref, live_ref, count_ref, hs_ref, q_ref, fresh_ref, pool_ref, up_ref, o_ref, ml_ref,
+    list_ref, hs_ref, q_ref, fresh_ref, pool_ref, up_ref, o_ref, ml_ref,
     kbuf, sbuf, sfresh, qp, acc, oacc, mbuf, lbuf, mlcol, upbuf, slot_of, page_sem, up_sem,
 ):
     prompts = list_ref.shape[0]
@@ -178,10 +241,10 @@
     me = lax.axis_index("seq")
 
     def page_copy(p, i, at):
-        return pltpu.make_async_copy(pool_ref.at[list_ref[p, i]], kbuf.at[at], page_sem.at[at])
+        return pltpu.make_async_copy(pool_ref.at[list_ref[p, 0, i]], kbuf.at[at], page_sem.at[at])
 
     def blocks_of(p):
-        return (count_ref[p] + block_pages - 1) // block_pages
+        return (list_ref[p, 2, 0] + block_pages - 1) // block_pages
 
     def start_prompt(p, base):
         count = blocks_of(p) * block_pages
@@ -234,7 +297,7 @@
             scores = jnp.dot(qp[...], keys, preferred_element_type=jnp.float32) * log2_scale
             top = mbuf[...]
             for i in range(block_pages):
-                live = live_ref[p, j * block_pages + i]
+                live = list_ref[p, 1, j * block_pages + i]
                 piece = jnp.where(lane < live, scores[:, i * 128 : (i + 1) * 128], floor_score)
                 sbuf[j, :, i * 128 : (i + 1) * 128] = piece
                 top = jnp.maximum(top, piece)
@@ -362,64 +425,54 @@
     value_up,
 ):
     n = lax.axis_size("seq")
-    me = lax.axis_index("seq")
+    big = pltpu.CompilerParams
     per_host, steps, heads, width = queries.shape
     latent = kv_gain.shape[0]
     vhead = value_up.shape[2]
     page_count, page_rows = cache_pool.shape[:2]
-    prompts, table_width = page_table.shape
+    prompts = page_table.shape[0]
     host_rows = per_host * steps * heads
     slot_rows = steps * heads
     slots = n * per_host
     rows = fork_count * slot_rows
-    local = page_table - me * page_count
-    owned = jnp.logical_and(local >= 0, local < page_count)
-    column = jnp.arange(table_width, dtype=jnp.int32)
-    before = column[None, :] < column[:, None]
-    rank = jnp.sum(
-        jnp.where(jnp.logical_and(before[None], owned[:, None, :]), 1, 0), axis=2, dtype=jnp.int32
-    )
-    list_width = -(-page_count // block_pages) * block_pages
-    order = jnp.arange(list_width, dtype=jnp.int32)
-    hot = jnp.logical_and(owned[:, None, :], rank[:, None, :] == order[None, :, None])
-    page_list = jnp.sum(jnp.where(hot, local[:, None, :], 0), axis=2, dtype=jnp.int32)
-    left = jnp.minimum(prompt_len[:, None] - column[None, :] * page_rows, page_rows)
-    page_live = jnp.sum(jnp.where(hot, left[:, None, :], 0), axis=2, dtype=jnp.int32)
-    counts = jnp.sum(owned, axis=1, dtype=jnp.int32)
-
-    hs_tile = jnp.pad(host_samples[None, :], ((0, 7), (0, 128 - per_host)))
-    hidden = jnp.pad(
-        new_hidden.reshape(per_host * steps, -1), ((0, 16 - per_host * steps), (0, 0))
-    )
-    big = pltpu.CompilerParams
-    qall, hsall, rows16 = pl.pallas_call(
-        functools.partial(gather_kernel, n),
+    list_width = -(-page_count // 128) * 128
+    qall, hsall, rows16, new_rows, lists = pl.pallas_call(
+        functools.partial(gather_kernel, n, page_count, page_rows),
         out_shape=(
             jax.ShapeDtypeStruct((n, host_rows, width), jnp.bfloat16),
             jax.ShapeDtypeStruct((n, 8, 128), jnp.int32),
             jax.ShapeDtypeStruct((16, width), jnp.bfloat16),
+            jax.ShapeDtypeStruct((per_host, steps, width), jnp.bfloat16),
+            jax.ShapeDtypeStruct((prompts, 8, list_width), jnp.int32),
         ),
-        in_specs=[vmem, vmem, vmem, anywhere, vmem],
-        out_specs=(vmem, vmem, vmem),
+        in_specs=[hbm, smem, vmem, hbm, vmem, vmem, smem],
+        out_specs=(hbm, hbm, hbm, vmem, hbm),
         scratch_shapes=[
             pltpu.VMEM(kv_down.shape[::-1], jnp.bfloat16),
             pltpu.VMEM((8, width), jnp.float32),
             pltpu.VMEM((8, width), jnp.float32),
+            pltpu.VMEM((8, kv_down.shape[0]), jnp.float32),
+            pltpu.VMEM((8, 128), jnp.int32),
+            pltpu.VMEM((16, width), jnp.bfloat16),
+            pltpu.VMEM((prompts, 8, list_width), jnp.int32),
             pltpu.SemaphoreType.DMA,
-            pltpu.SemaphoreType.DMA((2,)),
-            pltpu.SemaphoreType.DMA((n, 3)),
-            pltpu.SemaphoreType.DMA((n,)),
+            pltpu.SemaphoreType.DMA((4,)),
+            pltpu.SemaphoreType.DMA((n, 3, 2)),
+            pltpu.SemaphoreType.DMA((n, 2)),
             pltpu.SemaphoreType.DMA((n, 3)),
             pltpu.SemaphoreType.DMA((n,)),
             pltpu.SemaphoreType.DMA,
             pltpu.SemaphoreType.DMA,
         ],
         compiler_params=big(
-            collective_id=0, has_side_effects=True, vmem_limit_bytes=48 * 2**20
+            collective_id=0, has_side_effects=True, vmem_limit_bytes=20 * 2**20
         ),
-    )(queries.reshape(host_rows, width), hs_tile, hidden, kv_down.T, kv_gain[None, :])
-    new_rows = rows16[: per_host * steps].reshape(per_host, steps, width)
-
+    )(
+        queries.reshape(host_rows, width), host_samples, new_hidden, kv_down.T, kv_gain[None, :],
+        page_table, prompt_len,
+    )
+
+    score_blocks = -(-page_count // block_pages)
     slots_held = -(-page_count // block_pages) * block_pages + (block_pages - 1) * prompts
     o, ml = pl.pallas_call(
         attend_kernel,
@@ -427,11 +480,11 @@
             jax.ShapeDtypeStruct((slots, slot_rows, vhead), jnp.float32),
             jax.ShapeDtypeStruct((n, 8, 128), jnp.float32),
         ),
-        in_specs=[smem, smem, smem, smem, vmem, vmem, anywhere, anywhere],
+        in_specs=[smem, smem, vmem, vmem, hbm, hbm],
         out_specs=(vmem, vmem),
         scratch_shapes=[
             pltpu.VMEM((slots_held, width, page_rows), jnp.bfloat16),
-            pltpu.VMEM((list_width // block_pages, rows, block_pages * page_rows), jnp.float32),
+            pltpu.VMEM((score_blocks, rows, block_pages * page_rows), jnp.float32),
             pltpu.VMEM((rows, 16), jnp.float32),
             pltpu.VMEM((rows, width), jnp.bfloat16),
             pltpu.VMEM((latent // 128, rows, 128), jnp.float32),
@@ -444,9 +497,9 @@
             pltpu.SemaphoreType.DMA((slots_held,)),
             pltpu.SemaphoreType.DMA,
         ],
-        compiler_params=big(vmem_limit_bytes=60 * 2**20),
+        compiler_params=big(vmem_limit_bytes=(40 + slots // 8) * 2**20),
     )(
-        page_list, page_live, counts, hsall, qall.reshape(slots, slot_rows, width), rows16,
+        lists, hsall, qall.reshape(slots, slot_rows, width), rows16,
         jnp.swapaxes(cache_pool, 1, 2), value_up,
     )
 
@@ -465,7 +518,7 @@
             pltpu.SemaphoreType.DMA((n,)),
         ],
         compiler_params=big(
-            collective_id=1, has_side_effects=True, vmem_limit_bytes=48 * 2**20
+            collective_id=1, has_side_effects=True, vmem_limit_bytes=16 * 2**20
         ),
     )(o.reshape(n, host_rows, vhead), ml)
     return (new_rows, out.reshape(per_host, steps, heads, vhead))

time: 68.6 us -> 62 us (0.904)
  the two profiles are of different devices: /device:TPU:14 before, /device:TPU:0 now
where the time goes in v2:
time: 62 us; the launch traced here: 61.9 us
  Pallas kernels  53.2 us (86%)
  local copies, waits for them, and re-layouts  8.03 us (13%)
  between operations  0.69 us (1%)
    pallas_call x1, Pallas kernels, on_device(): pl.pallas_call(functools.partial(gather_kernel, n, page_count, page_rows)...  22.7 us
    pallas_call x1, Pallas kernels, on_device(): pl.pallas_call(attend_kernel, out_shape=(jax.ShapeDtypeStruct((slots, slo...  19 us
    pallas_call x1, Pallas kernels, on_device(): pl.pallas_call(functools.partial(combine_kernel, n), out_shape=jax.ShapeD...  11.5 us
    unnamed x18, local copies, waits for them, and re-layouts  8.03 us

profile of v2, /device:TPU:0, one launch (start us, length us, event | category | flops | bytes accessed | tf_op | source)
XLA Modules:
  0.0 61.9 jit_solution(17844360202186458182)
XLA Ops:
  0.6 0.0 copy-start
  0.6 0.0 copy-start.1
  0.7 2.3 %copy-done.1 = bf16[3584,576]{0,1:T(8,128)(2,1)S(1)} copy-done((bf16[3584,576]{0,1:T(8,128)(2,1)S(1)}, bf16[3584,576]{0,1:T(8,128)(2,1)}, u32[]{:S(2)}) %copy-start.1) | copy-done | bytes 4128792
  3.0 0.0 copy-start.2
  3.0 1.1 %copy-done.2 = bf16[2,2,32,576]{3,2,1,0:T(8,128)(2,1)S(1)} copy-done((bf16[2,2,32,576]{3,2,1,0:T(8,128)(2,1)S(1)}, bf16[2,2,32,576]{3,2,1,0:T(8,128)(2,1)}, u32[]{:S(2)}) %copy-start.2) | copy-done | bytes 147480
  4.1 0.0 copy-start.3
  4.1 0.7 %copy-done.3 = bf16[2,2,3584]{2,1,0:T(2,128)(2,1)S(1)} copy-done((bf16[2,2,3584]{2,1,0:T(2,128)(2,1)S(1)}, bf16[2,2,3584]{2,1,0:T(2,128)(2,1)}, u32[]{:S(2)}) %copy-start.3) | copy-done | bytes 28696
  4.8 0.0 copy-start.4
  4.8 0.7 %copy-done.4 = f32[512]{0:T(512)S(1)} copy-done((f32[512]{0:T(512)S(1)}, f32[512]{0:T(512)}, u32[]{:S(2)}) %copy-start.4) | copy-done | bytes 2072
  5.5 0.0 copy-start.5
  5.5 0.7 %copy-done.5 = s32[2,128]{1,0:T(2,128)S(1)} copy-done((s32[2,128]{1,0:T(2,128)S(1)}, s32[2,128]{1,0:T(2,128)}, u32[]{:S(2)}) %copy-start.5) | copy-done | bytes 1048
  6.2 0.0 copy-start.6
  6.2 0.7 %copy-done.6 = s32[2]{0:T(128)S(1)} copy-done((s32[2]{0:T(128)S(1)}, s32[2]{0:T(128)}, u32[]{:S(2)}) %copy-start.6) | copy-done | bytes 32
  6.8 0.0 copy-start.7
  6.8 0.7 %copy-done.7 = s32[2]{0:T(128)S(1)} copy-done((s32[2]{0:T(128)S(1)}, s32[2]{0:T(128)}, u32[]{:S(2)}) %copy-start.7) | copy-done | bytes 32
  7.5 22.7 %shard_map.104 = (bf16[8,128,576]{2,1,0:T(8,128)(2,1)S(1)}, s32[8,8,128]{2,1,0:T(8,128)S(1)}, bf16[16,576]{1,0:T(8,128)(2,1)S(1)}, bf16[2,2,576]{2,1,0:T(2,128)(2,1)S(1)}, s32[2,8,128]{2,1,0:T(8,128)S(1)}) custom-call(bf16[128,576]{1,0:T(8,128)(2,1)S(1)} %bitcast.10, s32[2]{0:T(128)S(1)} %copy-done.6, bf16[2,2,3584]{2,1,0:T(2,128)(2,1)S(1)} %copy-done.3, ...), custom_call_target="tpu_custom_call" | custom-call | tf_op jit(solution)/shard_map/pallas_call | solution.py:439
  30.2 0.0 copy-done
  30.2 19.0 %shard_map.105 = (f32[16,64,128]{2,1,0:T(8,128)S(1)}, f32[8,8,128]{2,1,0:T(8,128)S(1)}) custom-call(s32[2,8,128]{2,1,0:T(8,128)S(1)} %get-tuple-element.10.list_ref, s32[8,8,128]{2,1,0:T(8,128)S(1)} %get-tuple-element.11.hs_ref, bf16[16,64,576]{2,1,0:T(8,128)(2,1)S(1)} %bitcast.8, bf16[16,576]{1,0:T(8,128)(2,1)S(1)} %get-tuple-element.13.fresh_ref, ...), custom_call_target="tpu_custom_call" | custom-call | tf_op jit(solution)/shard_map/pallas_call | solution.py:477
  49.2 11.5 %shard_map.106 = bf16[128,128]{1,0:T(8,128)(2,1)S(1)} custom-call(f32[8,128,128]{2,1,0:T(8,128)S(1)} %bitcast.9, f32[8,8,128]{2,1,0:T(8,128)S(1)} %get-tuple-element.15.ml_ref), custom_call_target="tpu_custom_call" | custom-call | tf_op jit(solution)/shard_map/pallas_call | solution.py:506
  60.7 0.6 copy.13
  61.3 0.6 copy.14
Async XLA Ops:
  0.6 29.6 %copy-start = (bf16[32,512,128]{2,1,0:T(8,128)(2,1)S(1)}, bf16[32,512,128]{2,1,0:T(8,128)(2,1)}, u32[]{:S(2)}) copy-start(bf16[32,512,128]{2,1,0:T(8,128)(2,1)} %up_ref.1) | copy-start | bytes 12582916
  0.6 2.3 %copy-start.1 = (bf16[3584,576]{0,1:T(8,128)(2,1)S(1)}, bf16[3584,576]{0,1:T(8,128)(2,1)}, u32[]{:S(2)}) copy-start(bf16[3584,576]{0,1:T(8,128)(2,1)} %param.15) | copy-start | bytes 12386308
  3.0 1.1 %copy-start.2 = (bf16[2,2,32,576]{3,2,1,0:T(8,128)(2,1)S(1)}, bf16[2,2,32,576]{3,2,1,0:T(8,128)(2,1)}, u32[]{:S(2)}) copy-start(bf16[2,2,32,576]{3,2,1,0:T(8,128)(2,1)} %param.13) | copy-start | bytes 442372
  4.1 0.7 %copy-start.3 = (bf16[2,2,3584]{2,1,0:T(2,128)(2,1)S(1)}, bf16[2,2,3584]{2,1,0:T(2,128)(2,1)}, u32[]{:S(2)}) copy-start(bf16[2,2,3584]{2,1,0:T(2,128)(2,1)} %nh_ref.1) | copy-start | bytes 86020
  4.8 0.7 %copy-start.4 = (f32[512]{0:T(512)S(1)}, f32[512]{0:T(512)}, u32[]{:S(2)}) copy-start(f32[512]{0:T(512)} %param.16) | copy-start | bytes 6148
  5.5 0.7 %copy-start.5 = (s32[2,128]{1,0:T(2,128)S(1)}, s32[2,128]{1,0:T(2,128)}, u32[]{:S(2)}) copy-start(s32[2,128]{1,0:T(2,128)} %table_ref.1) | copy-start | bytes 3076
  6.2 0.7 %copy-start.6 = (s32[2]{0:T(128)S(1)}, s32[2]{0:T(128)}, u32[]{:S(2)}) copy-start(s32[2]{0:T(128)} %host_ref.1) | copy-start | bytes 28
  6.8 0.7 %copy-start.7 = (s32[2]{0:T(128)S(1)}, s32[2]{0:T(128)}, u32[]{:S(2)}) copy-start(s32[2]{0:T(128)} %len_ref.1) | copy-start | bytes 28

commit v3 on v2

--- a/solution.py
+++ b/solution.py
@@ -20,9 +20,9 @@
 
 
 def gather_kernel(
-    n, page_count, page_rows, q_ref, host_ref, nh_ref, down_ref, gain_ref, table_ref, len_ref,
+    n, page_count, page_rows, q_ref, host_ref, nh_hbm, down_ref, gain_hbm, table_hbm, len_ref,
     qall_ref, hsall_ref, rows_ref, new_ref, list_ref,
-    down_buf, raw_mine, raw_other, nh_buf, hs_ref, rows_buf, list_buf, down_sem, own_sem, q_send,
+    down_buf, nh_ref, gain_ref, table_ref, raw_mine, raw_other, nh_buf, hs_ref, rows_buf, new_buf, list_buf, down_sem, own_sem, q_send,
     q_recv, hs_send, hs_recv, raw_send, raw_recv,
 ):
     minor = 2
@@ -32,6 +32,13 @@
     head = lax.axis_index("head")
     half = q_ref.shape[0] // 2
     down_copy = pltpu.make_async_copy(down_ref, down_buf, down_sem)
+    small = []
+    for i, (source, target) in enumerate(
+        ((nh_hbm, nh_ref), (gain_hbm, gain_ref), (table_hbm, table_ref))
+    ):
+        copy = pltpu.make_async_copy(source, target, own_sem.at[5 + i])
+        copy.start()
+        small.append(copy)
     down_copy.start()
     barrier = pltpu.get_barrier_semaphore()
 
@@ -111,6 +118,8 @@
     own_q.start()
     own_hs.start()
     per_host, steps = nh_ref.shape[:2]
+    for copy in small:
+        copy.wait()
     nh_buf[...] = jnp.zeros_like(nh_buf)
     for i in range(per_host):
         nh_buf[i * steps : (i + 1) * steps, :] = nh_ref[i].astype(jnp.float32)
@@ -200,11 +209,12 @@
                 jnp.bfloat16
             )
             for i in range(per_host):
-                new_ref[i] = done[i * steps : (i + 1) * steps].astype(jnp.bfloat16)
+                new_buf[i] = done[i * steps : (i + 1) * steps].astype(jnp.bfloat16)
             page_lists()
             extra = [
                 pltpu.make_async_copy(rows_buf, rows_ref, own_sem.at[2]),
                 pltpu.make_async_copy(list_buf, list_ref, own_sem.at[3]),
+                pltpu.make_async_copy(new_buf, new_ref, own_sem.at[4]),
             ]
             for copy in extra:
                 copy.start()
@@ -230,8 +240,8 @@
 
 
 def attend_kernel(
-    list_ref, hs_ref, q_ref, fresh_ref, pool_ref, up_ref, o_ref, ml_ref,
-    kbuf, sbuf, sfresh, qp, acc, oacc, mbuf, lbuf, mlcol, upbuf, slot_of, page_sem, up_sem,
+    list_ref, hs_ref, q_hbm, fresh_hbm, new_in, pool_ref, up_ref, o_ref, ml_ref, new_out,
+    q_ref, fresh_ref, in_sem, kbuf, sbuf, sfresh, qp, acc, oacc, mbuf, lbuf, mlcol, upbuf, slot_of, page_sem, up_sem,
 ):
     prompts = list_ref.shape[0]
     per_host = 2
@@ -256,7 +266,15 @@
         lax.fori_loop(0, count, start_page, 0)
         return base + count
 
+    first = [
+        pltpu.make_async_copy(q_hbm, q_ref, in_sem.at[0]),
+        pltpu.make_async_copy(fresh_hbm, fresh_ref, in_sem.at[1]),
+    ]
+    for copy in first:
+        copy.start()
     lax.fori_loop(0, prompts, start_prompt, 0)
+    new_copy = pltpu.make_async_copy(new_in, new_out, in_sem.at[2])
+    new_copy.start()
     up_copy = pltpu.make_async_copy(up_ref, upbuf, up_sem)
     up_copy.start()
 
@@ -265,6 +283,8 @@
         return carry
 
     lax.fori_loop(0, slots, note_slot, 0)
+    for copy in first:
+        copy.wait()
     lane = lax.broadcasted_iota(jnp.int32, (1, 128), 1)
     fresh_lane = lax.broadcasted_iota(jnp.int32, (slot_rows, 16), 1)
     step_of = lax.broadcasted_iota(jnp.int32, (slot_rows, 16), 0) // heads
@@ -371,6 +391,7 @@
         return carry
 
     lax.fori_loop(0, slots // per_host, turn, 0)
+    new_copy.wait()
 
 
 def combine_kernel(
@@ -418,6 +439,46 @@
     for k in range(1, n):
         out = out + turned[:, k : k + 1] * o_got[k]
     out_ref[...] = out.astype(jnp.bfloat16)
+
+
+def attend(lists, hsall, qall, rows16, new_rows, pool, value_up):
+    n = hsall.shape[0]
+    prompts = lists.shape[0]
+    slots, slot_rows, width = qall.shape
+    heads, latent, vhead = value_up.shape
+    page_count, page_rows = pool.shape[0], pool.shape[2]
+    rows = fork_count * slot_rows
+    score_blocks = -(-page_count // block_pages)
+    slots_held = score_blocks * block_pages + (block_pages - 1) * prompts
+    return pl.pallas_call(
+        attend_kernel,
+        out_shape=(
+            jax.ShapeDtypeStruct((slots, slot_rows, vhead), jnp.float32),
+            jax.ShapeDtypeStruct((n, 8, 128), jnp.float32),
+            jax.ShapeDtypeStruct(new_rows.shape, jnp.bfloat16),
+        ),
+        in_specs=[smem, smem, hbm, hbm, hbm, hbm, hbm],
+        out_specs=(vmem, vmem, hbm),
+        scratch_shapes=[
+            pltpu.VMEM((slots, slot_rows, width), jnp.bfloat16),
+            pltpu.VMEM((16, width), jnp.bfloat16),
+            pltpu.SemaphoreType.DMA((3,)),
+            pltpu.VMEM((slots_held, width, page_rows), jnp.bfloat16),
+            pltpu.VMEM((score_blocks, rows, block_pages * page_rows), jnp.float32),
+            pltpu.VMEM((rows, 16), jnp.float32),
+            pltpu.VMEM((rows, width), jnp.bfloat16),
+            pltpu.VMEM((latent // 128, rows, 128), jnp.float32),
+            pltpu.VMEM((rows, vhead), jnp.float32),
+            pltpu.VMEM((rows, 128), jnp.float32),
+            pltpu.VMEM((rows, 128), jnp.float32),
+            pltpu.VMEM((slots, slot_rows, 128), jnp.float32),
+            pltpu.VMEM(value_up.shape, jnp.bfloat16),
+            pltpu.SMEM((slots,), jnp.int32),
+            pltpu.SemaphoreType.DMA((slots_held,)),
+            pltpu.SemaphoreType.DMA,
+        ],
+        compiler_params=pltpu.CompilerParams(vmem_limit_bytes=60 * 2**20),
+    )(lists, hsall, qall, rows16, new_rows, pool, value_up)
 
 
 def on_device(
@@ -445,18 +506,22 @@
             jax.ShapeDtypeStruct((per_host, steps, width), jnp.bfloat16),
             jax.ShapeDtypeStruct((prompts, 8, list_width), jnp.int32),
         ),
-        in_specs=[hbm, smem, vmem, hbm, vmem, vmem, smem],
-        out_specs=(hbm, hbm, hbm, vmem, hbm),
+        in_specs=[hbm, smem, hbm, hbm, hbm, hbm, smem],
+        out_specs=(hbm, hbm, hbm, hbm, hbm),
         scratch_shapes=[
             pltpu.VMEM(kv_down.shape[::-1], jnp.bfloat16),
+            pltpu.VMEM(new_hidden.shape, jnp.bfloat16),
+            pltpu.VMEM((1, latent), jnp.float32),
+            pltpu.VMEM(page_table.shape, jnp.int32),
             pltpu.VMEM((8, width), jnp.float32),
             pltpu.VMEM((8, width), jnp.float32),
             pltpu.VMEM((8, kv_down.shape[0]), jnp.float32),
             pltpu.VMEM((8, 128), jnp.int32),
             pltpu.VMEM((16, width), jnp.bfloat16),
+            pltpu.VMEM((per_host, steps, width), jnp.bfloat16),
             pltpu.VMEM((prompts, 8, list_width), jnp.int32),
             pltpu.SemaphoreType.DMA,
-            pltpu.SemaphoreType.DMA((4,)),
+            pltpu.SemaphoreType.DMA((8,)),
             pltpu.SemaphoreType.DMA((n, 3, 2)),
             pltpu.SemaphoreType.DMA((n, 2)),
             pltpu.SemaphoreType.DMA((n, 3)),
@@ -465,41 +530,15 @@
             pltpu.SemaphoreType.DMA,
         ],
         compiler_params=big(
-            collective_id=0, has_side_effects=True, vmem_limit_bytes=20 * 2**20
+            collective_id=0, has_side_effects=True, vmem_limit_bytes=62 * 2**20
         ),
     )(
         queries.reshape(host_rows, width), host_samples, new_hidden, kv_down.T, kv_gain[None, :],
         page_table, prompt_len,
     )
 
-    score_blocks = -(-page_count // block_pages)
-    slots_held = -(-page_count // block_pages) * block_pages + (block_pages - 1) * prompts
-    o, ml = pl.pallas_call(
-        attend_kernel,
-        out_shape=(
-            jax.ShapeDtypeStruct((slots, slot_rows, vhead), jnp.float32),
-            jax.ShapeDtypeStruct((n, 8, 128), jnp.float32),
-        ),
-        in_specs=[smem, smem, vmem, vmem, hbm, hbm],
-        out_specs=(vmem, vmem),
-        scratch_shapes=[
-            pltpu.VMEM((slots_held, width, page_rows), jnp.bfloat16),
-            pltpu.VMEM((score_blocks, rows, block_pages * page_rows), jnp.float32),
-            pltpu.VMEM((rows, 16), jnp.float32),
-            pltpu.VMEM((rows, width), jnp.bfloat16),
-            pltpu.VMEM((latent // 128, rows, 128), jnp.float32),
-            pltpu.VMEM((rows, vhead), jnp.float32),
-            pltpu.VMEM((rows, 128), jnp.float32),
-            pltpu.VMEM((rows, 128), jnp.float32),
-            pltpu.VMEM((slots, slot_rows, 128), jnp.float32),
-            pltpu.VMEM(value_up.shape, jnp.bfloat16),
-            pltpu.SMEM((slots,), jnp.int32),
-            pltpu.SemaphoreType.DMA((slots_held,)),
-            pltpu.SemaphoreType.DMA,
-        ],
-        compiler_params=big(vmem_limit_bytes=(40 + slots // 8) * 2**20),
-    )(
-        lists, hsall, qall.reshape(slots, slot_rows, width), rows16,
+    o, ml, new_rows = attend(
+        lists, hsall, qall.reshape(slots, slot_rows, width), rows16, new_rows,
         jnp.swapaxes(cache_pool, 1, 2), value_up,
     )
 

time: 62 us -> 57.9 us (0.934)
  the two profiles are of different devices: /device:TPU:0 before, /device:TPU:14 now
where the time goes in v3:
time: 57.9 us; the launch traced here: 57.1 us
  Pallas kernels  54 us (93%)
  local copies, waits for them, and re-layouts  2.41 us (4%)
  between operations  0.67 us (1%)
    pallas_call x1, Pallas kernels, on_device(): pl.pallas_call(functools.partial(gather_kernel, n, page_count, page_rows)...  19.2 us
    pallas_call x1, Pallas kernels, attend(): pl.pallas_call(attend_kernel, out_shape=(jax.ShapeDtypeStruct((slots, slo...  18.5 us
    pallas_call x1, Pallas kernels, on_device(): pl.pallas_call(functools.partial(combine_kernel, n), out_shape=jax.ShapeD...  16.4 us
    unnamed x5, local copies, waits for them, and re-layouts  2.41 us

profile of v3, /device:TPU:14, one launch (start us, length us, event | category | flops | bytes accessed | tf_op | source)
XLA Modules:
  0.0 57.1 jit_solution(3548208792509712349)
XLA Ops:
  0.6 19.2 %shard_map.104 = (bf16[8,128,576]{2,1,0:T(8,128)(2,1)}, s32[8,8,128]{2,1,0:T(8,128)}, bf16[16,576]{1,0:T(8,128)(2,1)}, bf16[2,2,576]{2,1,0:T(2,128)(2,1)}, s32[2,8,128]{2,1,0:T(8,128)}) custom-call(bf16[128,576]{1,0:T(8,128)(2,1)} %bitcast.12, s32[2]{0:T(128)} %host_ref.1, bf16[2,2,3584]{2,1,0:T(2,128)(2,1)} %nh_hbm.1, bf16[576,3584]{1,0:T(8,128)(2,1)} %bitcast.10, ...), custom_call_target="tpu_custom_call" | custom-call | tf_op jit(solution)/shard_map/pallas_call | solution.py:500
  19.8 18.5 %shard_map.105 = (f32[16,64,128]{2,1,0:T(8,128)}, f32[8,8,128]{2,1,0:T(8,128)}, bf16[2,2,576]{2,1,0:T(2,128)(2,1)}) custom-call(s32[2,8,128]{2,1,0:T(8,128)} %get-tuple-element.10.list_ref, s32[8,8,128]{2,1,0:T(8,128)} %get-tuple-element.11.hs_ref, bf16[16,64,576]{2,1,0:T(8,128)(2,1)} %bitcast.11, bf16[16,576]{1,0:T(8,128)(2,1)} %get-tuple-element.13.fresh_hbm, ...), custom_call_target="tpu_custom_call" | custom-call | tf_op jit(solution)/shard_map/pallas_call | solution.py:453
  38.3 0.0 copy-start
  38.3 1.0 %copy-done = f32[16,64,128]{2,1,0:T(8,128)S(1)} copy-done((f32[16,64,128]{2,1,0:T(8,128)S(1)}, f32[16,64,128]{2,1,0:T(8,128)}, u32[]{:S(2)}) %copy-start) | copy-done | bytes 524312
  39.4 0.0 copy-start.1
  39.4 0.8 %copy-done.1 = f32[8,8,128]{2,1,0:T(8,128)S(1)} copy-done((f32[8,8,128]{2,1,0:T(8,128)S(1)}, f32[8,8,128]{2,1,0:T(8,128)}, u32[]{:S(2)}) %copy-start.1) | copy-done | bytes 32792
  40.1 16.4 %shard_map.106 = bf16[128,128]{1,0:T(8,128)(2,1)S(1)} custom-call(f32[8,128,128]{2,1,0:T(8,128)S(1)} %bitcast.7, f32[8,8,128]{2,1,0:T(8,128)S(1)} %copy-done.1), custom_call_target="tpu_custom_call" | custom-call | tf_op jit(solution)/shard_map/pallas_call | solution.py:545
  56.5 0.6 %copy.12 = bf16[2,2,32,128]{3,2,1,0:T(8,128)(2,1)} copy(bf16[2,2,32,128]{3,2,1,0:T(8,128)(2,1)S(1)} %bitcast.8) | data formatting | bytes 65536
Async XLA Ops:
  38.3 1.0 %copy-start = (f32[16,64,128]{2,1,0:T(8,128)S(1)}, f32[16,64,128]{2,1,0:T(8,128)}, u32[]{:S(2)}) copy-start(f32[16,64,128]{2,1,0:T(8,128)} %get-tuple-element.16) | copy-start | bytes 1572868
  39.4 0.8 %copy-start.1 = (f32[8,8,128]{2,1,0:T(8,128)S(1)}, f32[8,8,128]{2,1,0:T(8,128)}, u32[]{:S(2)}) copy-start(f32[8,8,128]{2,1,0:T(8,128)} %get-tuple-element.17.ml_ref) | copy-start | bytes 98308

commit v4 on v3

--- a/solution.py
+++ b/solution.py
@@ -394,51 +394,108 @@
     new_copy.wait()
 
 
-def combine_kernel(
-    n, o_ref, ml_ref, out_ref, o_got, ml_got, gains, o_send, o_recv, ml_send, ml_recv
-):
-    me = lax.axis_index("seq")
-    barrier = pltpu.get_barrier_semaphore()
-    for k in range(1, n):
-        pl.semaphore_signal(
-            barrier, inc=1, device_id={"seq": (me + k) % n}, device_id_type=mesh_ids
-        )
-    pl.semaphore_wait(barrier, n - 1)
-    copies = []
-    for k in range(1, n):
-        dest = (me + k) % n
-        for src, got, s_sem, r_sem in (
-            (ml_ref, ml_got, ml_send, ml_recv),
-            (o_ref, o_got, o_send, o_recv),
-        ):
-            copy = pltpu.make_async_remote_copy(
-                src_ref=src.at[dest],
-                dst_ref=got.at[k],
-                send_sem=s_sem.at[k],
-                recv_sem=r_sem.at[k],
-                device_id={"seq": dest},
-                device_id_type=mesh_ids,
-            )
-            copy.start()
-            copies.append(copy)
-    ml_got[0] = ml_ref[me]
-    o_got[0] = o_ref[me]
-    for copy in copies:
-        copy.wait()
-    top = ml_got[0, 0:1, :]
-    for k in range(1, n):
-        top = jnp.maximum(top, ml_got[k, 0:1, :])
+def merge(blocks, ml_of, o_of, gains):
+    top = ml_of(0)[0:1]
+    for k in range(1, blocks):
+        top = jnp.maximum(top, ml_of(k)[0:1])
     total = jnp.zeros_like(top)
     gains[...] = jnp.zeros_like(gains)
-    for k in range(n):
-        factor = jnp.exp2(ml_got[k, 0:1, :] - top)
+    for k in range(blocks):
+        factor = jnp.exp2(ml_of(k)[0:1] - top)
         gains[k : k + 1, :] = factor
-        total = total + factor * ml_got[k, 1:2, :]
-    turned = (gains[...] / total).T
-    out = turned[:, 0:1] * o_got[0]
-    for k in range(1, n):
-        out = out + turned[:, k : k + 1] * o_got[k]
+        total = total + factor * ml_of(k)[1:2]
+    return top, total
+
+
+def weigh(blocks, turned, o_of):
+    out = turned[:, 0:1] * o_of(0)
+    for k in range(1, blocks):
+        out = out + turned[:, k : k + 1] * o_of(k)
+    return out
+
+
+def combine_kernel(
+    n, o_ref, ml_ref, out_ref, o_own, ml_own, o_mate, ml_mate, o_pair, ml_pair, o_got, ml_got,
+    gains, own_sem, mate_send, mate_recv, far_send, far_recv,
+):
+    minor = 2
+    major = n // minor
+    me = lax.axis_index("seq")
+    a, b = me // minor, me % minor
+    mate = a * minor + (1 - b)
+    barrier = pltpu.get_barrier_semaphore()
+    pl.semaphore_signal(barrier, inc=1, device_id={"seq": mate}, device_id_type=mesh_ids)
+    for k in range(1, major):
+        pl.semaphore_signal(
+            barrier, inc=1, device_id={"seq": (me + k * minor) % n}, device_id_type=mesh_ids
+        )
+    order = list(range(1, major)) + [0]
+    owns = []
+    for k in order:
+        place = (a + k) % major * minor + b
+        pair = [
+            pltpu.make_async_copy(ml_ref.at[place], ml_own.at[k], own_sem.at[k, 0]),
+            pltpu.make_async_copy(o_ref.at[place], o_own.at[k], own_sem.at[k, 1]),
+        ]
+        for copy in pair:
+            copy.start()
+        owns.append(pair)
+    pl.semaphore_wait(barrier, major)
+
+    def push(src, dst, sems, k, i, dest):
+        copy = pltpu.make_async_remote_copy(
+            src_ref=src,
+            dst_ref=dst,
+            send_sem=sems[0].at[k, i],
+            recv_sem=sems[1].at[k, i],
+            device_id={"seq": dest},
+            device_id_type=mesh_ids,
+        )
+        copy.start()
+        return copy
+
+    near = (mate_send, mate_recv)
+    far = (far_send, far_recv)
+    swaps = []
+    for k in order:
+        place = (a + k) % major * minor + (1 - b)
+        swaps.append(
+            [
+                push(ml_ref.at[place], ml_mate.at[k], near, k, 0, mate),
+                push(o_ref.at[place], o_mate.at[k], near, k, 1, mate),
+            ]
+        )
+    sent = []
+    line = lax.broadcasted_iota(jnp.int32, (8, 128), 0)
+    for at, k in enumerate(order):
+        for copy in owns[at]:
+            copy.wait()
+        for copy in swaps[at]:
+            copy.wait_recv()
+        ml_of = lambda i: (ml_own if i == 0 else ml_mate)[k]
+        o_of = lambda i: (o_own if i == 0 else o_mate)[k]
+        top, total = merge(2, ml_of, o_of, gains)
+        summed = weigh(2, gains[...].T, o_of)
+        both = jnp.where(line == 0, top, total)
+        if k == 0:
+            ml_got[0] = both
+            o_got[0] = summed
+        else:
+            ml_pair[k] = both
+            o_pair[k] = summed
+            dest = (me + k * minor) % n
+            sent.append(push(ml_pair.at[k], ml_got.at[k], far, k, 0, dest))
+            sent.append(push(o_pair.at[k], o_got.at[k], far, k, 1, dest))
+    for copy in sent:
+        copy.wait_recv()
+    top, total = merge(major, lambda i: ml_got[i], lambda i: o_got[i], gains)
+    out = weigh(major, (gains[...] / total).T, lambda i: o_got[i])
     out_ref[...] = out.astype(jnp.bfloat16)
+    for pair in swaps:
+        for copy in pair:
+            copy.wait_send()
+    for copy in sent:
+        copy.wait_send()
 
 
 def attend(lists, hsall, qall, rows16, new_rows, pool, value_up):
@@ -545,19 +602,23 @@
     out = pl.pallas_call(
         functools.partial(combine_kernel, n),
         out_shape=jax.ShapeDtypeStruct((host_rows, vhead), jnp.bfloat16),
-        in_specs=[vmem, vmem],
+        in_specs=[hbm, hbm],
         out_specs=vmem,
         scratch_shapes=[
-            pltpu.VMEM((n, host_rows, vhead), jnp.float32),
-            pltpu.VMEM((n, 8, 128), jnp.float32),
+            pltpu.VMEM((n // 2, lines, 128), jnp.float32)
+            for _ in range(4)
+            for lines in (host_rows, 8)
+        ]
+        + [
             pltpu.VMEM((128, 128), jnp.float32),
-            pltpu.SemaphoreType.DMA((n,)),
-            pltpu.SemaphoreType.DMA((n,)),
-            pltpu.SemaphoreType.DMA((n,)),
-            pltpu.SemaphoreType.DMA((n,)),
+            pltpu.SemaphoreType.DMA((n // 2, 2)),
+            pltpu.SemaphoreType.DMA((n // 2, 2)),
+            pltpu.SemaphoreType.DMA((n // 2, 2)),
+            pltpu.SemaphoreType.DMA((n // 2, 2)),
+            pltpu.SemaphoreType.DMA((n // 2, 2)),
         ],
         compiler_params=big(
-            collective_id=1, has_side_effects=True, vmem_limit_bytes=16 * 2**20
+            collective_id=1, has_side_effects=True, vmem_limit_bytes=62 * 2**20
         ),
     )(o.reshape(n, host_rows, vhead), ml)
     return (new_rows, out.reshape(per_host, steps, heads, vhead))

time: 57.9 us -> 56.1 us (0.969)
  the two profiles are of different devices: /device:TPU:14 before, /device:TPU:0 now
where the time goes in v4:
time: 56.1 us; the launch traced here: 56.4 us
  Pallas kernels  54.4 us (97%)
  local copies, waits for them, and re-layouts  1.38 us (2%)
  between operations  0.66 us (1%)
    pallas_call x1, Pallas kernels, on_device(): pl.pallas_call(functools.partial(gather_kernel, n, page_count, page_rows)...  23.6 us
    pallas_call x1, Pallas kernels, attend(): pl.pallas_call(attend_kernel, out_shape=(jax.ShapeDtypeStruct((slots, slo...  17.4 us
    pallas_call x1, Pallas kernels, on_device(): pl.pallas_call(functools.partial(combine_kernel, n), out_shape=jax.ShapeD...  13.3 us
    unnamed x1, local copies, waits for them, and re-layouts  1.38 us

profile of v4, /device:TPU:0, one launch (start us, length us, event | category | flops | bytes accessed | tf_op | source)
XLA Modules:
  0.0 56.4 jit_solution(2501939908333172743)
XLA Ops:
  0.6 23.6 %shard_map.104 = (bf16[8,128,576]{2,1,0:T(8,128)(2,1)}, s32[8,8,128]{2,1,0:T(8,128)}, bf16[16,576]{1,0:T(8,128)(2,1)}, bf16[2,2,576]{2,1,0:T(2,128)(2,1)}, s32[2,8,128]{2,1,0:T(8,128)}) custom-call(bf16[128,576]{1,0:T(8,128)(2,1)} %bitcast.11, s32[2]{0:T(128)} %host_ref.1, bf16[2,2,3584]{2,1,0:T(2,128)(2,1)} %nh_hbm.1, bf16[576,3584]{1,0:T(8,128)(2,1)} %bitcast.8, ...), custom_call_target="tpu_custom_call" | custom-call | tf_op jit(solution)/shard_map/pallas_call | solution.py:557
  24.3 17.4 %shard_map.105 = (f32[16,64,128]{2,1,0:T(8,128)}, f32[8,8,128]{2,1,0:T(8,128)}, bf16[2,2,576]{2,1,0:T(2,128)(2,1)}) custom-call(s32[2,8,128]{2,1,0:T(8,128)} %get-tuple-element.10.list_ref, s32[8,8,128]{2,1,0:T(8,128)} %get-tuple-element.11.hs_ref, bf16[16,64,576]{2,1,0:T(8,128)(2,1)} %bitcast.9, bf16[16,576]{1,0:T(8,128)(2,1)} %get-tuple-element.13.fresh_hbm, ...), custom_call_target="tpu_custom_call" | custom-call | tf_op jit(solution)/shard_map/pallas_call | solution.py:510
  41.7 13.3 %shard_map.106 = bf16[128,128]{1,0:T(8,128)(2,1)} custom-call(f32[8,128,128]{2,1,0:T(8,128)} %bitcast.10, f32[8,8,128]{2,1,0:T(8,128)} %get-tuple-element.17.ml_ref), custom_call_target="tpu_custom_call" | custom-call | tf_op jit(solution)/shard_map/pallas_call | solution.py:602
  55.0 1.4 %copy.12 = bf16[2,2,32,128]{3,2,1,0:T(8,128)(2,1)} copy(bf16[2,2,32,128]{3,2,1,0:T(8,128)(2,1)} %bitcast.12) | data formatting | bytes 65536
